TPU v7x, 32 devices: a whole 2x2x4 slice. The times are simulated.
32 devices in a mesh: grp: 4 (over y, x), swap: 8 (over z, core).
Axes of the slice: x: 2, y: 2, z: 4, core: 2. Of those that a mesh axis runs over, the one named last changes fastest.
Arguments:
- tokens: bfloat16 [4, 1024, 8, 512], P('grp', None, 'swap'), may hold values from -6 to 6
- sample_counts: int32 [4], P('grp'), may hold values from 1 to 1024, as said below
- feature_counts: int32 [4], P('grp'), may hold values from 1 to 8, as said below
- attn_in: bfloat16 [2, 512, 1536], replicated, may hold values from -0.25 to 0.25
- attn_out: bfloat16 [2, 512, 512], replicated, may hold values from -1.5 to 1.5
- norm_gain: float32 [3, 512], replicated, may hold values from 0.5 to 1.5
- norm_bias: float32 [3, 512], replicated, may hold values from -1.8 to 1.8
- mlp_in: bfloat16 [512, 2048], replicated, may hold values from -0.25 to 0.25
- mlp_in_bias: float32 [2048], replicated, may hold values from -1.8 to 1.8
- mlp_out: bfloat16 [2048, 512], replicated, may hold values from -0.125 to 0.125
- mlp_out_bias: float32 [512], replicated, may hold values from -1.8 to 1.8
- cotangent: bfloat16 [4, 1024, 8, 512], P('grp', None, 'swap'), may hold values from -6 to 6
Outputs:
- mixed: bfloat16 [4, 1024, 8, 512], P('grp', None, 'swap')
- tokens_grad: bfloat16 [4, 1024, 8, 512], P('grp', None, 'swap')
- attn_in_grad: float32 [2, 512, 1536], P(None, 'swap')
- attn_out_grad: float32 [2, 512, 512], P(None, 'swap')
- norm_gain_grad: float32 [3, 512], P(None, 'swap')
- norm_bias_grad: float32 [3, 512], P(None, 'swap')
- mlp_in_grad: float32 [512, 2048], P('swap')
- mlp_in_bias_grad: float32 [2048], P('swap')
- mlp_out_grad: float32 [2048, 512], P('swap')
- mlp_out_bias_grad: float32 [512], P('swap')
Inputs may be any that keep to these rules, and one draw needn't show every extreme that they name: `sample_counts`: the number of real samples of each task; in every draw one task has all 1024. `feature_counts`: the number of real features of each task; in every draw one task has all 8.
All inputs are finite; a program needn't handle non-finite values.
Results may differ from a plain program's by a relative error of at most 0.018.
Values may be sent and summed in bfloat16 or wider, within the bound.
A program may use at most 256 MiB of HBM per device.

v0:
```python
import jax
import jax.numpy as jnp
from jax import lax
from jax.sharding import PartitionSpec as P

HEADS = 8
HEAD_DIM = 64


EPSILON = 1e-05
MASKED = -1e30
SAMPLE_FORMS = ("tqfhe,tkfhe->tfhqk", "tfhqk,tkfhe->tqfhe", "tfhqk,tqfhe->tkfhe")
FEATURE_FORMS = ("tsqhe,tskhe->tshqk", "tshqk,tskhe->tsqhe", "tshqk,tsqhe->tskhe")


def layer_norm(values, factor, offset):
    centre = values - jnp.mean(values, axis=-1, keepdims=True)
    spread = jnp.mean(centre * centre, axis=-1, keepdims=True)
    return centre * lax.rsqrt(spread + EPSILON) * factor + offset


def exact_gelu(values):
    return jax.nn.gelu(values, approximate=False)


def project(left, weight):
    return jnp.dot(left, weight, preferred_element_type=jnp.float32)


def project_back(grad_rows, weight):
    return jnp.einsum("...c,dc->...d", grad_rows, weight, preferred_element_type=jnp.float32)


def weight_grad(left, grad_rows):
    return jnp.einsum(
        "nd,nc->dc",
        left.reshape(-1, left.shape[-1]),
        grad_rows.reshape(-1, grad_rows.shape[-1]),
        preferred_element_type=jnp.float32,
    )


def split_heads(packed):
    leading = packed.shape[:-1]
    model_width = packed.shape[-1] // 3
    query_rows = packed[..., :model_width].reshape(leading + (HEADS, HEAD_DIM))
    key_rows = packed[..., model_width : 2 * model_width].reshape(leading + (HEADS, HEAD_DIM))
    value_rows = packed[..., 2 * model_width :].reshape(leading + (HEADS, HEAD_DIM))
    return (query_rows, key_rows, value_rows)


def masked_scores(query_rows, key_rows, valid, forms):
    raw_scores = jnp.einsum(
        forms[0], query_rows, key_rows, preferred_element_type=jnp.float32
    ) * HEAD_DIM ** (-0.5)
    return jnp.where(valid[:, None, None, None, :], raw_scores, MASKED)


def attend(packed, valid, forms):
    leading = packed.shape[:-1]
    query_rows, key_rows, value_rows = split_heads(packed)
    scores = masked_scores(query_rows, key_rows, valid, forms)
    row_max = jnp.max(scores, axis=-1, keepdims=True)
    exponent = jnp.exp(scores - row_max)
    row_total = jnp.sum(exponent, axis=-1, keepdims=True)
    probability = (exponent / row_total).astype(jnp.bfloat16)
    mixed_rows = jnp.einsum(forms[1], probability, value_rows, preferred_element_type=jnp.float32)
    return (mixed_rows.reshape(leading + (packed.shape[-1] // 3,)), row_max + jnp.log(row_total))


def attend_back(packed, valid, log_total, grad_out, forms):
    leading = packed.shape[:-1]
    model_width = packed.shape[-1] // 3
    query_rows, key_rows, value_rows = split_heads(packed)
    grad_rows = grad_out.reshape(leading + (HEADS, HEAD_DIM))
    scores = masked_scores(query_rows, key_rows, valid, forms)
    probability = jnp.exp(scores - log_total)
    grad_values = jnp.einsum(
        forms[2], probability.astype(jnp.bfloat16), grad_rows, preferred_element_type=jnp.float32
    )
    grad_probs = jnp.einsum(forms[0], grad_rows, value_rows, preferred_element_type=jnp.float32)
    inner_sum = jnp.sum(probability * grad_probs, axis=-1, keepdims=True)
    grad_scores = (probability * (grad_probs - inner_sum)).astype(jnp.bfloat16)
    grad_query = jnp.einsum(
        forms[1], grad_scores, key_rows, preferred_element_type=jnp.float32
    ) * HEAD_DIM ** (-0.5)
    grad_keys = jnp.einsum(
        forms[2], grad_scores, query_rows, preferred_element_type=jnp.float32
    ) * HEAD_DIM ** (-0.5)
    return jnp.concatenate(
        [
            grad_query.reshape(leading + (model_width,)).astype(jnp.bfloat16),
            grad_keys.reshape(leading + (model_width,)).astype(jnp.bfloat16),
            grad_values.reshape(leading + (model_width,)).astype(jnp.bfloat16),
        ],
        axis=-1,
    )


def local(
    tokens,
    sample_counts,
    feature_counts,
    attn_in,
    attn_out,
    norm_gain,
    norm_bias,
    mlp_in,
    mlp_in_bias,
    mlp_out,
    mlp_out_bias,
    cotangent,
):
    samples = tokens.shape[1]
    sample_valid = jnp.arange(samples, dtype=jnp.int32)[None, :] < sample_counts[:, None]
    inputs = tokens.astype(jnp.float32)
    norm_one, back_one = jax.vjp(layer_norm, inputs, norm_gain[0], norm_bias[0])
    normed_one = norm_one.astype(jnp.bfloat16)
    packed_one = project(normed_one, attn_in[0]).astype(jnp.bfloat16)
    attn_one, log_total_one = attend(packed_one, sample_valid, SAMPLE_FORMS)
    attn_one = attn_one.astype(jnp.bfloat16)
    first_resid = (inputs + project(attn_one, attn_out[0])).astype(jnp.bfloat16)
    moved_rows = lax.all_to_all(first_resid, "swap", split_axis=1, concat_axis=2, tiled=True)
    features = moved_rows.shape[2]
    feature_valid = jnp.arange(features, dtype=jnp.int32)[None, :] < feature_counts[:, None]
    resid_one = moved_rows.astype(jnp.float32)
    norm_two, back_two = jax.vjp(layer_norm, resid_one, norm_gain[1], norm_bias[1])
    normed_two = norm_two.astype(jnp.bfloat16)
    packed_two = project(normed_two, attn_in[1]).astype(jnp.bfloat16)
    attn_two, log_total_two = attend(packed_two, feature_valid, FEATURE_FORMS)
    attn_two = attn_two.astype(jnp.bfloat16)
    resid_two = resid_one + project(attn_two, attn_out[1])
    norm_three, back_three = jax.vjp(layer_norm, resid_two, norm_gain[2], norm_bias[2])
    normed_three = norm_three.astype(jnp.bfloat16)
    hidden = project(normed_three, mlp_in) + mlp_in_bias
    activated, back_gelu = jax.vjp(exact_gelu, hidden)
    active_low = activated.astype(jnp.bfloat16)
    outcome = (resid_two + project(active_low, mlp_out) + mlp_out_bias).astype(jnp.bfloat16)
    mixed_out = lax.all_to_all(outcome, "swap", split_axis=2, concat_axis=1, tiled=True)
    grad_out = lax.all_to_all(cotangent, "swap", split_axis=1, concat_axis=2, tiled=True)
    grad_three = grad_out.astype(jnp.float32)
    grad_mlp_out = weight_grad(active_low, grad_out)
    grad_mlp_out_bias = jnp.sum(grad_three.reshape(-1, grad_three.shape[-1]), axis=0)
    grad_active = project_back(grad_out, mlp_out)
    grad_hidden = back_gelu(grad_active)[0].astype(jnp.bfloat16)
    grad_mlp_in = weight_grad(normed_three, grad_hidden)
    grad_mlp_in_bias = jnp.sum(
        grad_hidden.astype(jnp.float32).reshape(-1, grad_hidden.shape[-1]), axis=0
    )
    grad_resid, gain_three, offset_three = back_three(project_back(grad_hidden, mlp_in))
    grad_second = grad_three + grad_resid
    grad_second_low = grad_second.astype(jnp.bfloat16)
    grad_attn_out_two = weight_grad(attn_two, grad_second_low)
    grad_attn_two = project_back(grad_second_low, attn_out[1]).astype(jnp.bfloat16)
    grad_packed_two = attend_back(
        packed_two, feature_valid, log_total_two, grad_attn_two, FEATURE_FORMS
    )
    grad_attn_in_two = weight_grad(normed_two, grad_packed_two)
    grad_resid_two, gain_two, offset_two = back_two(project_back(grad_packed_two, attn_in[1]))
    grad_first = (grad_second + grad_resid_two).astype(jnp.bfloat16)
    grad_back = lax.all_to_all(grad_first, "swap", split_axis=2, concat_axis=1, tiled=True)
    grad_attn_out_one = weight_grad(attn_one, grad_back)
    grad_attn_one = project_back(grad_back, attn_out[0]).astype(jnp.bfloat16)
    grad_packed_one = attend_back(
        packed_one, sample_valid, log_total_one, grad_attn_one, SAMPLE_FORMS
    )
    grad_attn_in_one = weight_grad(normed_one, grad_packed_one)
    grad_input, gain_one, offset_one = back_one(project_back(grad_packed_one, attn_in[0]))
    tokens_grad = (grad_back.astype(jnp.float32) + grad_input).astype(jnp.bfloat16)
    stack_in = jnp.stack([grad_attn_in_one, grad_attn_in_two])
    stack_out = jnp.stack([grad_attn_out_one, grad_attn_out_two])
    stack_gain = jnp.stack([gain_one, gain_two, gain_three])
    stack_offset = jnp.stack([offset_one, offset_two, offset_three])
    (
        part_in,
        part_out,
        part_gain,
        part_offset,
        part_mlp_in,
        part_mlp_in_bias,
        part_mlp_out,
        part_mlp_out_bias,
    ) = (
        lax.psum_scatter(stack_in, "swap", scatter_dimension=1, tiled=True),
        lax.psum_scatter(stack_out, "swap", scatter_dimension=1, tiled=True),
        lax.psum_scatter(stack_gain, "swap", scatter_dimension=1, tiled=True),
        lax.psum_scatter(stack_offset, "swap", scatter_dimension=1, tiled=True),
        lax.psum_scatter(grad_mlp_in, "swap", scatter_dimension=0, tiled=True),
        lax.psum_scatter(grad_mlp_in_bias, "swap", scatter_dimension=0, tiled=True),
        lax.psum_scatter(grad_mlp_out, "swap", scatter_dimension=0, tiled=True),
        lax.psum_scatter(grad_mlp_out_bias, "swap", scatter_dimension=0, tiled=True),
    )
    (
        share_in,
        share_out,
        share_gain,
        share_offset,
        share_mlp_in,
        share_mlp_in_bias,
        share_mlp_out,
        share_mlp_out_bias,
    ) = (
        lax.psum(part_in.astype(jnp.bfloat16), "grp").astype(jnp.float32),
        lax.psum(part_out.astype(jnp.bfloat16), "grp").astype(jnp.float32),
        lax.psum(part_gain.astype(jnp.bfloat16), "grp").astype(jnp.float32),
        lax.psum(part_offset.astype(jnp.bfloat16), "grp").astype(jnp.float32),
        lax.psum(part_mlp_in.astype(jnp.bfloat16), "grp").astype(jnp.float32),
        lax.psum(part_mlp_in_bias.astype(jnp.bfloat16), "grp").astype(jnp.float32),
        lax.psum(part_mlp_out.astype(jnp.bfloat16), "grp").astype(jnp.float32),
        lax.psum(part_mlp_out_bias.astype(jnp.bfloat16), "grp").astype(jnp.float32),
    )
    return (
        mixed_out,
        tokens_grad,
        share_in,
        share_out,
        share_gain,
        share_offset,
        share_mlp_in,
        share_mlp_in_bias,
        share_mlp_out,
        share_mlp_out_bias,
    )


def solution(mesh):
    placed = (
        P("grp", None, "swap", None),
        P("grp"),
        P("grp"),
        P(),
        P(),
        P(),
        P(),
        P(),
        P(),
        P(),
        P(),
        P("grp", None, "swap", None),
    )
    return jax.shard_map(
        local,
        mesh=mesh,
        in_specs=placed,
        out_specs=(
            P("grp", None, "swap", None),
            P("grp", None, "swap", None),
            P(None, "swap", None),
            P(None, "swap", None),
            P(None, "swap"),
            P(None, "swap"),
            P("swap", None),
            P("swap"),
            P("swap", None),
            P("swap"),
        ),
        check_vma=False,
    )
```

profile of v0, /device:TPU:0, one launch (start us, length us, event | category | flops | bytes accessed | tf_op | source)
XLA Modules:
  0.0 687.2 jit_solution(9975648898985909655)
XLA Ops:
  12.0 9.0 %reduce.50 = bf16[1024,512]{1,0:T(8,128)(2,1)} reduce(bf16[1024,1,1,512]{3,2,1,0:T(2,128)(2,1)} %bitcast.267, bf16[]{:T(256)} %broadcast.407), dimensions={1,2}, to_apply=%bitcast.245.reduce_sub_computation | reduce | bytes 2097154
  23.8 6.7 all-to-all-start.2
  45.0 15.1 %fusion.103 = (f32[8,1024]{1,0:T(8,128)S(1)}, f32[8,1024,1024]{1,2,0:T(8,128)}) fusion(bf16[1024,8,64]{0,2,1:T(8,128)(2,1)} %bitcast.264, bf16[1024,8,64]{0,2,1:T(8,128)(2,1)} %bitcast.262, pred[1024]{0:T(1024)(128)(4,1)S(1)} %iota_compare_fusion), kind=kOutput, calls=%fused_computation.177 | convolution fusion | flops 1098899456 | bytes 35685376 | tf_op jit(solution)/shard_map/tqfhe,tkfhe->tfhqk/dot_general | solution.py:53
  60.1 13.1 %fusion.1 = f32[8,1024]{1,0:T(8,128)S(1)} fusion(f32[8,1024,1024]{1,2,0:T(8,128)} %get-tuple-element.50, f32[8,1024]{1,0:T(8,128)S(1)} %get-tuple-element.49), kind=kLoop, calls=%fused_computation.7 | loop fusion | flops 16769024 | bytes 33619968 | tf_op jit(solution)/shard_map/reduce_sum | solution.py:65
  73.2 13.9 %fusion.53 = bf16[8,64,1024]{2,1,0:T(8,128)(2,1)S(1)} fusion(bf16[1024,8,64]{0,2,1:T(8,128)(2,1)S(1)} %bitcast.272, f32[8,1024,1024]{1,2,0:T(8,128)} %get-tuple-element.50, f32[8,1024]{1,0:T(8,128)S(1)} %fusion.1, f32[8,1024]{1,0:T(8,128)S(1)} %get-tuple-element.49), kind=kOutput, calls=%fused_computation.107 | convolution fusion | flops 1099431936 | bytes 35717120 | tf_op jit(solution)/shard_map/tfhqk,tkfhe->tqfhe/dot_general | solution.py:67
  91.1 8.0 %reduce.49 = bf16[1024,512]{1,0:T(8,128)(2,1)S(1)} reduce(bf16[1024,1,1,512]{3,2,1,0:T(2,128)(2,1)} %bitcast.268, bf16[]{:T(256)} %broadcast.407), dimensions={1,2}, to_apply=%bitcast.246.reduce_sub_computation | reduce | bytes 2097154
  100.7 5.6 all-to-all-start
  107.0 5.8 reshape.833
  114.6 18.3 %all-to-all-done = bf16[8,2,32768]{2,1,0:T(2,128)(2,1)} async-done(((bf16[8,2,32768]{2,1,0:T(2,128)(2,1)}), bf16[8,2,32768]{2,1,0:T(2,128)(2,1)}, u32[]{:S(2)}, u32[]{:S(2)}) %all-to-all-start) | async-done | bytes 1048608 | tf_op jit(solution)/shard_map/all_to_all | solution.py:123
  132.9 5.8 reshape.831
  167.2 4.7 copy.163
  172.0 5.5 fusion.105
  187.2 4.8 convert_bitcast_fusion.1
  203.9 20.4 %multiply_convert_fusion.1 = (bf16[128,8,2048]{2,0,1:T(8,128)(2,1)}, f32[128,8,2048]{2,0,1:T(8,128)}) fusion(f32[128,8,2048]{2,0,1:T(8,128)S(1)} %get-tuple-element.53, f32[2048]{0:T(1024)S(1)} %copy-done.53, u8[128,2048]{1,0:T(8,128)(4,1)S(1)} %get-tuple-element.11, u8[128,2048]{1,0:T(8,128)(4,1)S(1)} %get-tuple-element.10), kind=kLoop, calls=%fused_computation.21 | loop fusion | flops 148897792 | bytes 21504000 | tf_op jit(solution)/shard_map/convert_element_type | solution.py:137
  224.3 8.1 %convert_reduce_fusion = (f32[2048]{0:T(1024)}, bf16[128,8,2048]{2,0,1:T(8,128)(2,1)S(1)}) fusion(f32[128,8,2048]{2,0,1:T(8,128)} %get-tuple-element.34, bf16[128,8,512]{2,0,1:T(8,128)(2,1)S(1)} %bitcast.257, bf16[2048,512]{1,0:T(8,128)(2,1)S(1)} %copy-done.65, f32[128,8,2048]{2,0,1:T(8,128)S(1)} %get-tuple-element.53, f32[2048]{0:T(1024)S(1)} %copy-done.53), kind=kOutput, calls=%fused_computation.19 | convolution fusion | flops 2183133184 | bytes 24133632 | tf_op jit(solution)/shard_map/...c,dc->...d/dot_general | solution.py:31
  242.8 4.9 copy.170
  247.7 4.8 fusion.106
  308.4 23.2 %all-to-all-done.3 = bf16[1,128,8,512]{3,1,0,2:T(8,128)(2,1)} async-done(((bf16[1,128,8,512]{3,1,0,2:T(8,128)(2,1)}), bf16[1,128,8,512]{3,1,0,2:T(8,128)(2,1)}, u32[]{:S(2)}, u32[]{:S(2)}) %all-to-all-start.3) | async-done | bytes 1048608 | tf_op jit(solution)/shard_map/all_to_all | solution.py:161
  335.7 8.0 %fusion.13 = f32[2048,512]{1,0:T(8,128)} fusion(bf16[128,8,2048]{2,0,1:T(8,128)(2,1)} %get-tuple-element.33, bf16[1,128,8,1,512]{4,1,2,3,0:T(8,128)(2,1)S(1)} %bitcast.260), kind=kOutput, calls=%fused_computation.35 | convolution fusion | flops 2147483648 | bytes 9437184 | tf_op jit(solution)/shard_map/nd,nc->dc/dot_general | solution.py:35
  344.6 5.7 convolution_bitcast_fusion
  357.4 22.7 %multiply_reduce_fusion = (f32[8,1024]{1,0:T(8,128)S(1)}, f32[8,1024,1024]{1,2,0:T(8,128)}) fusion(f32[8,1024,1024]{1,2,0:T(8,128)} %get-tuple-element.50, f32[8,1024]{1,0:T(8,128)S(1)} %log_add_fusion, bf16[1024,8,64]{0,2,1:T(8,128)(2,1)S(1)} %bitcast.270, bf16[1024,8,64]{0,2,1:T(8,128)(2,1)S(1)} %bitcast.273), kind=kOutput, calls=%fused_computation.2 | convolution fusion | flops 1098899456 | bytes 69271552 | tf_op jit(solution)/shard_map/tqfhe,tkfhe->tfhqk/dot_general | solution.py:81
  380.1 28.9 %multiply_convert_fusion = bf16[8,1024,1024]{1,2,0:T(8,128)(2,1)} fusion(f32[8,1024,1024]{1,2,0:T(8,128)} %get-tuple-element.57, f32[8,1024,1024]{1,2,0:T(8,128)} %get-tuple-element.50, f32[8,1024]{1,0:T(8,128)S(1)} %get-tuple-element.56, f32[8,1024]{1,0:T(8,128)S(1)} %log_add_fusion), kind=kLoop, calls=%fused_computation.1 | loop fusion | flops 33554432 | bytes 83951616 | tf_op jit(solution)/shard_map/convert_element_type | solution.py:83
  409.0 12.2 %multiply_convert_fusion.4 = bf16[8,64,1024]{2,1,0:T(8,128)(2,1)} fusion(bf16[1024,8,64]{0,2,1:T(8,128)(2,1)S(1)} %bitcast.265, bf16[8,1024,1024]{1,2,0:T(8,128)(2,1)} %multiply_convert_fusion), kind=kOutput, calls=%fused_computation.80 | convolution fusion | flops 1074790400 | bytes 18874368 | tf_op jit(solution)/shard_map/tfhqk,tqfhe->tkfhe/dot_general | solution.py:87
  421.2 9.9 %multiply_convert_fusion.5 = bf16[8,64,1024]{2,1,0:T(8,128)(2,1)} fusion(bf16[1024,8,64]{0,2,1:T(8,128)(2,1)S(1)} %bitcast.263, bf16[8,1024,1024]{1,2,0:T(8,128)(2,1)} %multiply_convert_fusion), kind=kOutput, calls=%fused_computation.81 | convolution fusion | flops 1074790400 | bytes 18874368 | tf_op jit(solution)/shard_map/tfhqk,tkfhe->tqfhe/dot_general | solution.py:84
  431.1 15.0 %fusion.50 = bf16[8,64,1024]{2,1,0:T(8,128)(2,1)} fusion(bf16[1024,8,64]{0,2,1:T(8,128)(2,1)S(1)} %bitcast.271, f32[8,1024,1024]{1,2,0:T(8,128)} %get-tuple-element.50, f32[8,1024]{1,0:T(8,128)S(1)} %log_add_fusion), kind=kOutput, calls=%fused_computation.104 | convolution fusion | flops 1091043328 | bytes 35684352 | tf_op jit(solution)/shard_map/tfhqk,tqfhe->tkfhe/dot_general | solution.py:78
  455.1 6.2 fusion.58
  465.7 4.9 fusion.28
  480.7 67.4 %reduce-scatter.11.cloned.1.call-done = f32[2,64,1536]{2,1,0:T(8,128)} async-done(((f32[2,512,1536]{2,1,0:T(8,128)}), f32[2,64,1536]{2,1,0:T(8,128)}) %reduce-scatter.11.cloned.1.call-update) | async-done | bytes 786448 | tf_op jit(solution)/shard_map/reduce_scatter | solution.py:184
  552.2 27.3 %all-reduce.2 = (bf16[2048]{0:T(1024)(128)(2,1)S(1)}, bf16[512]{0:T(512)(128)(2,1)S(1)}) all-reduce(f32[2048]{0:T(1024)S(1)} %copy-done.54, f32[512]{0:T(512)S(1)} %convert_reduce_fusion.2), channel_id=7, replica_groups=mesh['grp'=4,'swap'=8] {'swap'}, use_global_device_ids=true, to_apply=%region_35.36.clone | all-reduce | flops 2560 | bytes 15360
  584.9 30.6 %reduce-scatter.21.cloned.1.call-done = f32[64,3]{1,0:T(8,128)} async-done(((f32[512,3]{1,0:T(8,128)}), f32[64,3]{1,0:T(8,128)}) %reduce-scatter.21.cloned.1.call-update) | async-done | bytes 784
  616.3 9.9 %all-reduce.3 = (bf16[3,64]{1,0:T(4,128)(2,1)S(1)}, bf16[3,64]{1,0:T(4,128)(2,1)S(1)}, bf16[256]{0:T(256)(128)(2,1)S(1)}, bf16[64]{0:T(256)(128)(2,1)S(1)}) all-reduce(bf16[3,64]{1,0:T(4,128)(2,1)S(1)} %copy.202, bf16[3,64]{1,0:T(4,128)(2,1)S(1)} %copy.204, ...), channel_id=1, replica_groups=mesh['grp'=4,'swap'=8] {'grp'}, use_global_device_ids=true, to_apply=%region_26.27 | all-reduce | flops 704 | bytes 2816 | tf_op jit(solution)/shard_map/psum | solution.py:205
  628.5 42.8 %all-reduce.7.cloned.1.call-done = (bf16[2,64,1536]{2,1,0:T(8,128)(2,1)}, bf16[2,64,512]{2,1,0:T(8,128)(2,1)}, bf16[64,2048]{1,0:T(8,128)(2,1)}, bf16[256,512]{1,0:T(8,128)(2,1)}) async-done(((bf16[2,64,1536]{2,1,0:T(8,128)(2,1)}, bf16[2,64,512]{2,1,0:T(8,128)(2,1)}, bf16[64,2048]{1,0:T(8,128)(2,1)}, bf16[256,512]{1,0:T(8,128)(2,1)}), (bf16[2,64,1536]{2,1,0:T(8,128)(2,1)}, bf16[2,64,512]{2,1,0:T(8,128)(2,1)}, ...) | async-done | bytes 1048592 | tf_op jit(solution)/shard_map/psum | solution.py:203
  (265 shorter events, 200.0 us)
Async XLA Ops:
  7.2 192.1 %copy-start = (bf16[512,2048]{1,0:T(8,128)(2,1)S(1)}, bf16[512,2048]{1,0:T(8,128)(2,1)}, u32[]{:S(2)}) copy-start(bf16[512,2048]{1,0:T(8,128)(2,1)} %param.19) | copy-start | bytes 6291460
  21.0 10.1 %copy-start.12 = (bf16[1,1024,1,512]{3,1,2,0:T(8,128)(2,1)S(1)}, bf16[1,1024,1,512]{3,1,2,0:T(8,128)(2,1)}, u32[]{:S(2)}) copy-start(bf16[1,1024,1,512]{3,1,2,0:T(8,128)(2,1)} %param.12) | copy-start | bytes 3145732
  23.8 77.0 %all-to-all-start.2 = ((bf16[8,2,32768]{2,1,0:T(2,128)(2,1)}), bf16[8,2,32768]{2,1,0:T(2,128)(2,1)}, u32[]{:S(2)}, u32[]{:S(2)}) async-start(bf16[8,2,32768]{2,1,0:T(2,128)(2,1)} %reshape.832), calls=%async_computation.2 | async-start | bytes 2097152 | tf_op jit(solution)/shard_map/all_to_all | solution.py:140
  32.5 113.3 %copy-start.47 = (f32[1,512]{1,0:T(1,128)}, f32[1,512]{1,0:T(1,128)S(1)}, u32[]{:S(2)}) copy-start(f32[1,512]{1,0:T(1,128)S(1)} %get-tuple-element.45) | copy-start | bytes 6148
  33.1 112.7 %copy-start.63 = (f32[1,512]{1,0:T(1,128)}, f32[1,512]{1,0:T(1,128)S(1)}, u32[]{:S(2)}) copy-start(f32[1,512]{1,0:T(1,128)S(1)} %get-tuple-element.48) | copy-start | bytes 6148
  60.1 13.1 %copy-start.26 = (f32[8,1024]{1,0:T(8,128)}, f32[8,1024]{1,0:T(8,128)S(1)}, u32[]{:S(2)}) copy-start(f32[8,1024]{1,0:T(8,128)S(1)} %get-tuple-element.49) | copy-start | bytes 98308
  60.1 13.1 %copy-start.21 = (bf16[1,1024,1,512]{1,3,2,0:T(8,128)(2,1)S(1)}, bf16[1,1024,1,512]{1,3,2,0:T(8,128)(2,1)}, u32[]{:S(2)}) copy-start(bf16[1,1024,1,512]{1,3,2,0:T(8,128)(2,1)} %copy.152) | copy-start | bytes 3145732
  73.2 14.0 %copy-start.33 = (f32[8,1024]{1,0:T(8,128)}, f32[8,1024]{1,0:T(8,128)S(1)}, u32[]{:S(2)}) copy-start(f32[8,1024]{1,0:T(8,128)S(1)} %fusion.1) | copy-start | bytes 98308
  73.2 14.0 %copy-start.28 = (bf16[2,512,512]{2,1,0:T(8,128)(2,1)S(1)}, bf16[2,512,512]{2,1,0:T(8,128)(2,1)}, u32[]{:S(2)}) copy-start(bf16[2,512,512]{2,1,0:T(8,128)(2,1)} %param.16) | copy-start | bytes 3145732
  100.7 32.2 %all-to-all-start = ((bf16[8,2,32768]{2,1,0:T(2,128)(2,1)}), bf16[8,2,32768]{2,1,0:T(2,128)(2,1)}, u32[]{:S(2)}, u32[]{:S(2)}) async-start(bf16[8,2,32768]{2,1,0:T(2,128)(2,1)} %reshape.830), calls=%async_computation | async-start | bytes 2097152 | tf_op jit(solution)/shard_map/all_to_all | solution.py:123
  107.0 74.6 %copy-start.57 = (pred[8]{0:T(512)(128)(4,1)}, pred[8]{0:T(512)(128)(4,1)S(1)}, u32[]{:S(2)}) copy-start(pred[8]{0:T(512)(128)(4,1)S(1)} %iota_compare_fusion.1) | copy-start | bytes 28
  198.8 37.0 %copy-start.4 = (f32[128,8,512]{2,0,1:T(8,128)}, f32[128,8,512]{2,0,1:T(8,128)S(1)}, u32[]{:S(2)}) copy-start(f32[128,8,512]{2,0,1:T(8,128)S(1)} %get-tuple-element.52) | copy-start | bytes 6291460
  203.9 20.4 %copy-start.65 = (bf16[2048,512]{1,0:T(8,128)(2,1)S(1)}, bf16[2048,512]{1,0:T(8,128)(2,1)}, u32[]{:S(2)}) copy-start(bf16[2048,512]{1,0:T(8,128)(2,1)} %param.21) | copy-start | bytes 6291460
  300.8 30.8 %all-to-all-start.3 = ((bf16[1,128,8,512]{3,1,0,2:T(8,128)(2,1)}), bf16[1,128,8,512]{3,1,0,2:T(8,128)(2,1)}, u32[]{:S(2)}, u32[]{:S(2)}) async-start(bf16[1,128,8,512]{3,1,0,2:T(8,128)(2,1)} %fusion.66), calls=%async_computation.3 | async-start | bytes 2097152 | tf_op jit(solution)/shard_map/all_to_all | solution.py:161
  305.1 170.4 %reduce-scatter.13.cloned.1.call-start = ((), (), s32[]{:S(2)}) async-start(), calls=%async_computation.11 | async-start | bytes 2359296 | tf_op jit(solution)/shard_map/reduce_scatter | solution.py:185
  335.5 141.6 %reduce-scatter.17.cloned.1.call-start = ((), (), s32[]{:S(2)}) async-start(), calls=%async_computation.13 | async-start | bytes 4718592 | tf_op jit(solution)/shard_map/reduce_scatter | solution.py:190
  343.8 135.1 %reduce-scatter.15.cloned.1.call-start = ((), (), s32[]{:S(2)}) async-start(), calls=%async_computation.12 | async-start | bytes 4718592 | tf_op jit(solution)/shard_map/reduce_scatter | solution.py:188
  355.0 193.2 %reduce-scatter.11.cloned.1.call-start = ((), (), s32[]{:S(2)}) async-start(), calls=%async_computation.10 | async-start | bytes 7077888 | tf_op jit(solution)/shard_map/reduce_scatter | solution.py:184
  357.4 22.7 %copy-start.19 = (bf16[1024,512]{0,1:T(8,128)(2,1)}, bf16[1024,512]{0,1:T(8,128)(2,1)S(1)}, u32[]{:S(2)}) copy-start(bf16[1024,512]{0,1:T(8,128)(2,1)S(1)} %convolution_convert_fusion.2) | copy-start | bytes 3145732
  380.1 28.9 %copy-start.15 = (bf16[1,1024,1,512]{1,3,2,0:T(8,128)(2,1)S(1)}, bf16[1,1024,1,512]{1,3,2,0:T(8,128)(2,1)}, u32[]{:S(2)}) copy-start(bf16[1,1024,1,512]{1,3,2,0:T(8,128)(2,1)} %copy.153) | copy-start | bytes 3145732
  409.0 12.2 %copy-start.14 = (bf16[1,1024,1,512]{1,3,2,0:T(8,128)(2,1)S(1)}, bf16[1,1024,1,512]{1,3,2,0:T(8,128)(2,1)}, u32[]{:S(2)}) copy-start(bf16[1,1024,1,512]{1,3,2,0:T(8,128)(2,1)} %copy.154) | copy-start | bytes 3145732
  431.1 15.0 %copy-start.13 = (bf16[1,1024,1,512]{3,1,2,0:T(8,128)(2,1)S(1)}, bf16[1,1024,1,512]{3,1,2,0:T(8,128)(2,1)}, u32[]{:S(2)}) copy-start(bf16[1,1024,1,512]{3,1,2,0:T(8,128)(2,1)} %param.12) | copy-start | bytes 3145732
  431.1 15.0 %copy-start.36 = (f32[1024]{0:T(1024)S(1)}, f32[1024]{0:T(1024)}, u32[]{:S(2)}) copy-start(f32[1024]{0:T(1024)} %copy-done.35) | copy-start | bytes 12292
  431.1 15.0 %copy-start.38 = (f32[1024]{0:T(1024)S(1)}, f32[1024]{0:T(1024)}, u32[]{:S(2)}) copy-start(f32[1024]{0:T(1024)} %copy-done.37) | copy-start | bytes 12292
  431.1 15.0 %copy-start.50 = (f32[1,512]{1,0:T(1,128)S(1)}, f32[1,512]{1,0:T(1,128)}, u32[]{:S(2)}) copy-start(f32[1,512]{1,0:T(1,128)} %copy-done.49) | copy-start | bytes 6148
  431.1 15.0 %copy-start.62 = (f32[1,512]{1,0:T(1,128)S(1)}, f32[1,512]{1,0:T(1,128)}, u32[]{:S(2)}) copy-start(f32[1,512]{1,0:T(1,128)} %copy-done.61) | copy-start | bytes 6148
  461.4 118.3 %all-to-all-start.1 = ((bf16[1,128,8,512]{3,1,0,2:T(8,128)(2,1)}), bf16[1,128,8,512]{3,1,0,2:T(8,128)(2,1)}, u32[]{:S(2)}, u32[]{:S(2)}) async-start(bf16[1,128,8,512]{3,1,0,2:T(8,128)(2,1)} %fusion.58), calls=%async_computation.1 | async-start | bytes 2097152 | tf_op jit(solution)/shard_map/all_to_all | solution.py:139
  465.6 118.5 %reduce-scatter.19.cloned.1.call-start = ((), (), s32[]{:S(2)}) async-start(), calls=%async_computation.14 | async-start | bytes 294912
  474.4 141.0 %reduce-scatter.21.cloned.1.call-start = ((), (), s32[]{:S(2)}) async-start(), calls=%async_computation.15 | async-start | bytes 294912
  475.4 74.7 %copy-start.68 = (u32[32]{0:T(128)S(1)}, u32[32]{0:T(128)}, u32[]{:S(2)}) copy-start(u32[32]{0:T(128)} %constant.99) | copy-start | bytes 388
  475.4 195.8 %all-reduce.7.cloned.1.call-start = ((), (), s32[]{:S(2)}) async-start(), calls=%async_computation.16 | async-start | bytes 2097152 | tf_op jit(solution)/shard_map/psum | solution.py:203
  478.9 73.3 %copy-start.54 = (f32[2048]{0:T(1024)S(1)}, f32[2048]{0:T(1024)}, u32[]{:S(2)}) copy-start(f32[2048]{0:T(1024)} %get-tuple-element.60) | copy-start | bytes 24580
  (48 other events, 163.3 us)
Sparse Core Ops, SparseCore 0:
  335.6 34.6 reduce-scatter.12
  372.6 48.7 reduce-scatter.16
  423.7 48.2 reduce-scatter.14
  474.1 73.9 reduce-scatter.10
  550.8 33.2 reduce-scatter.18
  586.9 28.5 reduce-scatter.20
  619.9 51.3 all-reduce.6
where the time goes:
time: 696 us; the launch traced here: 687 us
  matrix products  188 us (27%)
  waiting for transfers between devices  184 us (26%)
  local copies, waits for them, and re-layouts  122 us (18%)
  other arithmetic  117 us (17%)
  blocking collectives  37.3 us (5%)
  starting transfers between devices  21.4 us (3%)
  between operations  18.1 us (3%)
    reduce_scatter x1, waiting for transfers between devices, local(): lax.psum_scatter(stack_in, 'swap', scatter_dimension=1, tiled=True)  67.4 us
    psum x1, waiting for transfers between devices, local(): lax.psum(part_in.astype(jnp.bfloat16), 'grp').astype(jnp.float32)  42.8 us
    unnamed x154, local copies, waits for them, and re-layouts  38.1 us
    unnamed x9, waiting for transfers between devices  32.1 us
    convert_element_type x1, other arithmetic, attend_back(): grad_scores = (probability * (grad_probs - inner_sum)).astype(jnp.bfloat16)  28.9 us
    dot_general x6, matrix products, weight_grad(): jnp.einsum('nd,nc->dc', left.reshape(-1, left.shape[-1]), grad_rows.resha...  28.2 us
    dot_general x2, matrix products, attend_back(): jnp.einsum(forms[0], grad_rows, value_rows, preferred_element_type=jnp.fl...  27.4 us
    unnamed x1, blocking collectives  27.3 us
  transfers between devices with their start and end apart: 11, of which 6 were waited for; matrix products, arithmetic and copies ran while one was open for 33% of the time, Pallas kernels for 0%

commit v1 on v0

--- a/solution.py
+++ b/solution.py
@@ -1,6 +1,8 @@
 import jax
 import jax.numpy as jnp
 from jax import lax
+from jax.experimental import pallas as pl
+from jax.experimental.pallas import tpu as pltpu
 from jax.sharding import PartitionSpec as P
 
 HEADS = 8
@@ -223,6 +225,834 @@
     )
 
 
+MESH = pl.DeviceIdType.MESH
+VMEM_LIMIT = 60 * 1024 * 1024
+SCALE = HEAD_DIM ** (-0.5)
+LOG2E = 1.4426950408889634
+LN2 = 0.6931471805599453
+BF = jnp.bfloat16
+F32 = jnp.float32
+NT = (((1,), (1,)), ((), ()))
+NN = (((1,), (0,)), ((), ()))
+TN = (((0,), (0,)), ((), ()))
+CHUNKS = 4
+BLOCK = 256
+SWAP = 8
+GRP = 4
+PIECE = BLOCK // SWAP
+PAIRS = 4
+WIDTH = 512
+MID_ROWS = 192
+END_ROWS = 64
+
+
+def mm(left, right, form=NN):
+    return lax.dot_general(left, right, form, preferred_element_type=F32)
+
+
+def norm_stats(values):
+    centre = values - jnp.mean(values, axis=-1, keepdims=True)
+    inverse = lax.rsqrt(jnp.mean(centre * centre, axis=-1, keepdims=True) + EPSILON)
+    return centre * inverse, inverse
+
+
+def norm_back(grad, vhat, inverse, gain):
+    scaled = grad * gain
+    mean_one = jnp.mean(scaled, axis=-1, keepdims=True)
+    mean_two = jnp.mean(scaled * vhat, axis=-1, keepdims=True)
+    return inverse * (scaled - mean_one - vhat * mean_two)
+
+
+def lanes(rows=BLOCK):
+    return lax.broadcasted_iota(jnp.int32, (rows, 128), 1)
+
+
+def split_three(values):
+    high = values.astype(BF).astype(F32)
+    rest = values - high
+    middle = rest.astype(BF).astype(F32)
+    low = rest - middle
+    place = lanes(values.shape[0]) & 63
+    terms = jnp.where(place == 0, high, jnp.where(place == 1, middle, jnp.where(place == 2, low, 0.0)))
+    return terms.astype(BF)
+
+
+def attention_forward(query, key, value, bias, put):
+    def score(head):
+        raw = mm(query(head // 2), key(head), NT)
+        return raw if bias is None else raw + bias
+
+    current = score(0)
+    for pair in range(PAIRS):
+        total = None
+        tops = []
+        for half in range(2):
+            head = 2 * pair + half
+            following = score(head + 1) if head + 1 < HEADS else None
+            top = jnp.max(current, axis=-1, keepdims=True)
+            weight = jnp.exp2(current - top).astype(BF)
+            term = mm(weight, value(head))
+            total = term if total is None else total + term
+            tops.append(top)
+            current = following
+        row_total = total[:, 128:]
+        out = (total[:, :128] / row_total).astype(BF)
+        top_pair = jnp.where(lanes() < 64, tops[0], tops[1])
+        put(pair, out, split_three(-(top_pair + jnp.log(row_total) * LOG2E)))
+
+
+def attention_back(query, grad, key, value, bias):
+    left = lanes() < 64
+    grad_query = grad_key = grad_value = None
+    for half in range(2):
+        keys = key(half)
+        score = mm(query, keys, NT)
+        if bias is not None:
+            score = score + bias
+        weight = jnp.exp2(score)
+        slope = mm(grad, value(half), NT)
+        grad_score = (weight * slope).astype(BF)
+        weight = weight.astype(BF)
+        mine = left if half == 0 else jnp.logical_not(left)
+        nothing = jnp.zeros((BLOCK, 128), BF)
+        terms = (
+            mm(grad_score, keys[:, :128]),
+            mm(grad_score, jnp.where(mine, query[:, :128], nothing), TN),
+            mm(weight, jnp.where(mine, grad[:, :128], nothing), TN),
+        )
+        if half == 0:
+            grad_query, grad_key, grad_value = terms
+        else:
+            grad_query, grad_key, grad_value = (
+                grad_query + terms[0],
+                grad_key + terms[1],
+                grad_value + terms[2],
+            )
+    return grad_query, grad_key, grad_value
+
+
+def fused_kernel(
+    tokens,
+    cotangent,
+    sample_counts,
+    feature_counts,
+    attn_in_hbm,
+    attn_out_hbm,
+    norm_gain,
+    norm_bias,
+    mlp_in_hbm,
+    mlp_in_bias,
+    mlp_out_hbm,
+    mlp_out_bias,
+    mixed,
+    tokens_grad,
+    mid_out,
+    end_out,
+    gain_out,
+    offset_out,
+    hidden_bias_out,
+    out_bias_out,
+    attn_in,
+    attn_out,
+    mlp_in,
+    mlp_out,
+    x_rows,
+    normed_one,
+    query_one,
+    key_one,
+    value_one,
+    ones_key,
+    ones_value,
+    attn_one,
+    first_send,
+    first_recv,
+    cot_recv,
+    grad_recv,
+    normed_two,
+    attn_two,
+    normed_three,
+    active,
+    grad_hidden,
+    grad_packed,
+    grad_low,
+    query_two,
+    key_two,
+    value_two,
+    feature_bias,
+    key_zero,
+    grad_key,
+    grad_value,
+    head_sum,
+    vectors,
+    vec_pair,
+    vec_grp,
+    vec_z,
+    mid_part,
+    mid_one,
+    mid_two,
+    mid_three,
+    mid_done,
+    load_sem,
+    first_ss,
+    first_rs,
+    cot_ss,
+    cot_rs,
+    mixed_ss,
+    mixed_rs,
+    grad_ss,
+    grad_rs,
+    out_sem,
+    mid_ss,
+    mid_rs,
+    end_ss,
+    end_rs,
+    vec_ss,
+    vec_rs,
+):
+    grp = lax.axis_index("grp")
+    me = lax.axis_index("swap")
+    chip = me // 2
+    core = me % 2
+    samples = sample_counts[0]
+    features = feature_counts[0]
+
+    def swap_peer(k):
+        return (me + k) % SWAP
+
+    def grp_peer(k):
+        return (grp + k) % GRP
+
+    def z_peer(k):
+        return ((chip + k) % 4) * 2 + core
+
+    loads = [pltpu.make_async_copy(tokens.at[:, c], x_rows.at[c], load_sem.at[c]) for c in range(CHUNKS)]
+    for index, (source, target) in enumerate(
+        (
+            (attn_in_hbm.at[0], attn_in.at[0]),
+            (attn_out_hbm.at[0], attn_out.at[0]),
+            (attn_in_hbm.at[1], attn_in.at[1]),
+            (attn_out_hbm.at[1], attn_out.at[1]),
+            (mlp_in_hbm, mlp_in),
+            (mlp_out_hbm, mlp_out),
+        )
+    ):
+        loads.append(pltpu.make_async_copy(source, target, load_sem.at[CHUNKS + index]))
+    for copy in loads:
+        copy.start()
+
+    barrier = pltpu.get_barrier_semaphore()
+    for k in range(1, SWAP):
+        pl.semaphore_signal(barrier, inc=1, device_id={"swap": swap_peer(k)}, device_id_type=MESH)
+    for k in range(1, GRP):
+        pl.semaphore_signal(barrier, inc=1, device_id={"grp": grp_peer(k)}, device_id_type=MESH)
+    pl.semaphore_wait(barrier, SWAP - 1 + GRP - 1)
+
+    def exchange(source, target, send, recv):
+        def copy(c, d, peer):
+            return pltpu.make_async_remote_copy(
+                src_ref=source(c, d),
+                dst_ref=target(c, peer),
+                send_sem=send.at[c, d],
+                recv_sem=recv.at[c, peer],
+                device_id={"swap": d},
+                device_id_type=MESH,
+            )
+
+        def start(c):
+            for k in range(1, SWAP):
+                copy(c, swap_peer(k), me).start()
+
+        def wait_send(c):
+            for k in range(1, SWAP):
+                copy(c, swap_peer(k), me).wait_send()
+
+        def wait_recv(c):
+            for k in range(1, SWAP):
+                copy(c, swap_peer(k), swap_peer(k)).wait_recv()
+
+        return start, wait_send, wait_recv
+
+    first_start, first_wait_send, first_wait_recv = exchange(
+        lambda c, d: first_send.at[c, d], lambda c, d: first_recv.at[c, d], first_ss, first_rs
+    )
+    cot_start, cot_wait_send, cot_wait_recv = exchange(
+        lambda c, d: cotangent.at[d, c], lambda c, d: cot_recv.at[c, d], cot_ss, cot_rs
+    )
+    mixed_start, mixed_wait_send, mixed_wait_recv = exchange(
+        lambda c, d: first_send.at[c, d], lambda c, d: mixed.at[d, c], mixed_ss, mixed_rs
+    )
+    grad_start, grad_wait_send, grad_wait_recv = exchange(
+        lambda c, d: first_recv.at[c, d], lambda c, d: grad_recv.at[c, d], grad_ss, grad_rs
+    )
+
+    def own_cot(c):
+        return pltpu.make_async_copy(cotangent.at[me, c], cot_recv.at[c, me], cot_rs.at[c, me])
+
+    def own_mixed(c):
+        return pltpu.make_async_copy(first_send.at[c, me], mixed.at[me, c], mixed_rs.at[c, me])
+
+    def cot_begin(c):
+        own_cot(c).start()
+        cot_start(c)
+
+    cot_begin(0)
+
+    vectors[...] = jnp.zeros((16, WIDTH), F32)
+    low_half = lax.broadcasted_iota(jnp.int32, (CHUNKS, BLOCK, 128), 2) < 64
+    ones_key[0] = jnp.where(low_half, 1.0, 0.0).astype(BF)
+    ones_key[1] = jnp.where(low_half, 0.0, 1.0).astype(BF)
+    head_sum[...] = jnp.where(
+        ((lax.broadcasted_iota(jnp.int32, (256, 128), 0) // 64) & 1)
+        == (lax.broadcasted_iota(jnp.int32, (256, 128), 1) // 64),
+        1.0,
+        0.0,
+    ).astype(BF)
+    row_cell = lax.broadcasted_iota(jnp.int32, (BLOCK, BLOCK), 0)
+    col_cell = lax.broadcasted_iota(jnp.int32, (BLOCK, BLOCK), 1)
+    seen = jnp.logical_and((row_cell % PIECE) == (col_cell % PIECE), (col_cell // PIECE) < features)
+    feature_bias[...] = jnp.where(seen, 0.0, MASKED).astype(F32)
+
+    def valid_rows(c):
+        row = lax.broadcasted_iota(jnp.int32, (BLOCK, 1), 0)
+        return (row // PIECE) * (CHUNKS * PIECE) + c * PIECE + row % PIECE < samples
+
+    def half_of(values, half):
+        mine = (lanes(values.shape[0]) < 64) == (half == 0)
+        return jnp.where(mine, values, jnp.zeros_like(values))
+
+    def add_row(row, values):
+        vectors[row : row + 1, :] += jnp.sum(values, axis=0, keepdims=True)
+
+    def block(ref, c):
+        return ref[c].reshape(BLOCK, WIDTH)
+
+    loads[CHUNKS].wait()
+
+    @pl.loop(0, CHUNKS)
+    def _(c):
+        pltpu.make_async_copy(tokens.at[:, c], x_rows.at[c], load_sem.at[c]).wait()
+        vhat, _ = norm_stats(block(x_rows, c).astype(F32))
+        normed = (vhat * norm_gain[0:1, :] + norm_bias[0:1, :]).astype(BF)
+        normed_one[c] = normed
+        valid = valid_rows(c)
+        queries = mm(normed, attn_in[0, :, :WIDTH]) * (SCALE * LOG2E)
+        for pair in range(PAIRS):
+            query_one[c, pair, :, :128] = queries[:, 128 * pair : 128 * pair + 128].astype(BF)
+        keys = mm(normed, attn_in[0, :, WIDTH : 2 * WIDTH])
+
+        @pl.when(c == 0)
+        def _():
+            key_zero[...] = keys[0:8, :]
+
+        keys = jnp.where(valid, keys, key_zero[0:1, :]).astype(BF)
+        values = mm(normed, attn_in[0, :, 2 * WIDTH :])
+        values = jnp.where(valid, values, 0.0).astype(BF)
+        for head in range(HEADS):
+            pair, half = head // 2, head % 2
+            cut = slice(128 * pair, 128 * pair + 128)
+            key_one[head, c] = half_of(keys[:, cut], half)
+            value_one[head, c] = half_of(values[:, cut], half)
+        for half in range(2):
+            mine = (lanes() < 64) == (half == 0)
+            ones_value[half, c] = jnp.where(jnp.logical_and(mine, valid), 1.0, 0.0).astype(BF)
+
+    cells = CHUNKS * BLOCK
+
+    def key_all(head):
+        return key_one[head].reshape(cells, 128)
+
+    def key_wide(head):
+        return jnp.concatenate([key_all(head), ones_key[head % 2].reshape(cells, 128)], axis=1)
+
+    def value_wide(head):
+        return jnp.concatenate(
+            [value_one[head].reshape(cells, 128), ones_value[head % 2].reshape(cells, 128)], axis=1
+        )
+
+    loads[CHUNKS + 1].wait()
+
+    @pl.loop(0, CHUNKS)
+    def _(c):
+        def put(pair, out, extra):
+            attn_one[c, :, 128 * pair : 128 * pair + 128] = out
+            query_one[c, pair, :, 128:] = extra
+
+        attention_forward(
+            lambda pair: query_one[c, pair, :, :128], key_all, value_wide, None, put
+        )
+        first = block(x_rows, c).astype(F32) + mm(attn_one[c], attn_out[0])
+        first_send[c] = first.astype(BF).reshape(SWAP, PIECE, WIDTH)
+        first_recv[c, me] = first_send[c, me]
+        first_start(c)
+
+        @pl.when(c < CHUNKS - 1)
+        def _():
+            cot_begin(c + 1)
+
+    for index in range(2, 6):
+        loads[CHUNKS + index].wait()
+
+    def delta_of(grad, out):
+        product = grad.astype(F32) * out.astype(F32)
+        high = product.astype(BF)
+        low = (product - high.astype(F32)).astype(BF)
+        return split_three(-mm(jnp.concatenate([high, low], axis=1), head_sum[...]))
+
+    @pl.loop(0, CHUNKS)
+    def _(c):
+        first_wait_recv(c)
+        resid_one = block(first_recv, c).astype(F32)
+        vhat_two, inverse_two = norm_stats(resid_one)
+        normed = (vhat_two * norm_gain[1:2, :] + norm_bias[1:2, :]).astype(BF)
+        normed_two[c] = normed
+        queries = mm(normed, attn_in[1, :, :WIDTH]) * (SCALE * LOG2E)
+        keys = mm(normed, attn_in[1, :, WIDTH : 2 * WIDTH]).astype(BF)
+        values = mm(normed, attn_in[1, :, 2 * WIDTH :]).astype(BF)
+        for pair in range(PAIRS):
+            cut = slice(128 * pair, 128 * pair + 128)
+            query_two[pair, :, :128] = queries[:, cut].astype(BF)
+            for half in range(2):
+                key_two[2 * pair + half, :, :128] = half_of(keys[:, cut], half)
+                key_two[2 * pair + half, :, 128:] = ones_key[half, 0]
+                value_two[2 * pair + half, :, :128] = half_of(values[:, cut], half)
+                value_two[2 * pair + half, :, 128:] = ones_key[half, 0]
+
+        def put(pair, out, extra):
+            attn_two[c, :, 128 * pair : 128 * pair + 128] = out
+            query_two[pair, :, 128:] = extra
+
+        attention_forward(
+            lambda pair: query_two[pair, :, :128],
+            lambda head: key_two[head, :, :128],
+            lambda head: value_two[head],
+            feature_bias[...],
+            put,
+        )
+        second = resid_one + mm(attn_two[c], attn_out[1])
+        vhat_three, inverse_three = norm_stats(second)
+        normed = (vhat_three * norm_gain[2:3, :] + norm_bias[2:3, :]).astype(BF)
+        normed_three[c] = normed
+        own_cot(c).wait()
+        cot_wait_recv(c)
+        cot_low = block(cot_recv, c)
+        cot = cot_low.astype(F32)
+        add_row(10, cot)
+        outcome = second + mlp_out_bias[...]
+        grad_normed = jnp.zeros((BLOCK, WIDTH), F32)
+        for part in range(4):
+            cut = slice(WIDTH * part, WIDTH * part + WIDTH)
+            hidden = mm(normed, mlp_in[:, cut]) + mlp_in_bias[:, cut]
+            weight_out = mlp_out[part].reshape(WIDTH, WIDTH)
+            grad_active = mm(cot_low, weight_out, NT)
+            below = 0.5 + 0.5 * lax.erf(hidden * 0.7071067811865476)
+            act = (hidden * below).astype(BF)
+            density = jnp.exp2(hidden * hidden * (-0.5 * LOG2E)) * 0.3989422804014327
+            grad_hid = ((below + hidden * density) * grad_active).astype(BF)
+            active[part, c] = act
+            grad_hidden[part, c] = grad_hid.reshape(GRP, END_ROWS, WIDTH)
+            add_row(6 + part, grad_hid.astype(F32))
+            outcome = outcome + mm(act, weight_out)
+            grad_normed = grad_normed + mm(grad_hid, mlp_in[:, cut], NT)
+        first_wait_send(c)
+        first_send[c] = outcome.astype(BF).reshape(SWAP, PIECE, WIDTH)
+        add_row(2, grad_normed * vhat_three)
+        add_row(5, grad_normed)
+        grad_second = cot + norm_back(grad_normed, vhat_three, inverse_three, norm_gain[2:3, :])
+        grad_second_low = grad_second.astype(BF)
+        grad_low[c] = grad_second_low
+        grad_attn = mm(grad_second_low, attn_out[1], NT).astype(BF)
+        for pair in range(PAIRS):
+            cut = slice(128 * pair, 128 * pair + 128)
+            piece = grad_attn[:, cut]
+            wide = jnp.concatenate([piece, delta_of(piece, attn_two[c, :, cut])], axis=1)
+            grad_q, grad_k, grad_v = attention_back(
+                query_two[pair],
+                wide,
+                lambda half: key_two[2 * pair + half],
+                lambda half: value_two[2 * pair + half],
+                feature_bias[...],
+            )
+            grad_packed[c, :, 128 * pair : 128 * pair + 128] = (grad_q * SCALE).astype(BF)
+            grad_packed[c, :, WIDTH + 128 * pair : WIDTH + 128 * pair + 128] = (grad_k * LN2).astype(BF)
+            grad_packed[c, :, 2 * WIDTH + 128 * pair : 2 * WIDTH + 128 * pair + 128] = grad_v.astype(BF)
+        grad_normed = mm(grad_packed[c], attn_in[1], NT)
+        add_row(1, grad_normed * vhat_two)
+        add_row(4, grad_normed)
+        grad_first = grad_second + norm_back(grad_normed, vhat_two, inverse_two, norm_gain[1:2, :])
+        first_recv[c] = grad_first.astype(BF).reshape(SWAP, PIECE, WIDTH)
+        grad_recv[c, me] = first_recv[c, me]
+        grad_start(c)
+        own_mixed(c).start()
+        mixed_start(c)
+
+    def rows_of(ref):
+        return ref[...].reshape(cells, WIDTH)
+
+    def shares(values, rows):
+        return values.astype(BF).reshape(4, 2, GRP, rows, WIDTH)
+
+    for part in range(4):
+        cut = slice(WIDTH * part, WIDTH * part + WIDTH)
+        tile = mm(rows_of(normed_three), grad_hidden[part].reshape(cells, WIDTH), TN)
+        mid_part[:, :, :, 16 * part : 16 * part + 16, :] = shares(tile, 16)
+        tile = mm(active[part].reshape(cells, WIDTH), rows_of(cot_recv), TN)
+        mid_part[part, :, :, 64:128, :] = tile.astype(BF).reshape(2, GRP, 64, WIDTH)
+    for part in range(3):
+        cut = slice(WIDTH * part, WIDTH * part + WIDTH)
+        tile = mm(rows_of(normed_two), grad_packed[:, :, cut].reshape(cells, WIDTH), TN)
+        mid_part[:, :, :, 128 + 16 * part : 144 + 16 * part, :] = shares(tile, 16)
+    tile = mm(rows_of(attn_two), rows_of(grad_low), TN)
+    mid_part[:, :, :, 176:192, :] = shares(tile, 16)
+
+    def reduction(part, one, two, three, done, out, send, recv):
+        def remote(source, target, index, where):
+            return pltpu.make_async_remote_copy(
+                src_ref=source,
+                dst_ref=target,
+                send_sem=send.at[index],
+                recv_sem=recv.at[index],
+                device_id=where,
+                device_id_type=MESH,
+            )
+
+        step_one = [remote(part.at[:, 1 - core], one, 0, {"swap": me + 1 - 2 * core})]
+        step_two = [
+            remote(one.at[:, grp_peer(k)], two.at[k - 1], k, {"grp": grp_peer(k)}) for k in range(1, GRP)
+        ]
+        step_three = [
+            remote(one.at[(chip + k) % 4, grp], three.at[k - 1], 3 + k, {"swap": z_peer(k)}) for k in range(1, 4)
+        ]
+        step_four = [remote(done, out.at[grp], 6 + k, {"grp": grp_peer(k)}) for k in range(1, GRP)]
+        own = pltpu.make_async_copy(done, out.at[grp], recv.at[10])
+
+        def begin():
+            for copy in step_one:
+                copy.start()
+
+        def after_one():
+            for copy in step_one:
+                copy.wait_recv()
+
+            @pl.loop(0, 4)
+            def _(a):
+                one[a] = (one[a].astype(F32) + part[a, core].astype(F32)).astype(BF)
+
+            for copy in step_two:
+                copy.start()
+
+        def after_two():
+            for copy in step_two:
+                copy.wait_recv()
+
+            @pl.loop(0, 4)
+            def _(a):
+                total = one[a, grp].astype(F32)
+                for k in range(3):
+                    total = total + two[k, a].astype(F32)
+                one[a, grp] = total.astype(BF)
+
+            for copy in step_three:
+                copy.start()
+
+        def after_three():
+            for copy in step_three:
+                copy.wait_recv()
+            total = one[chip, grp].astype(F32)
+            for k in range(3):
+                total = total + three[k].astype(F32)
+            done[...] = total.astype(BF)
+            own.start()
+            for copy in step_four:
+                copy.start()
+
+        def finish():
+            own.wait()
+            for copy in step_four:
+                copy.wait_recv()
+            for copy in step_one + step_two + step_three + step_four:
+                copy.wait_send()
+
+        return begin, after_one, after_two, after_three, finish
+
+    mid = reduction(mid_part, mid_one, mid_two, mid_three, mid_done, mid_out, mid_ss, mid_rs)
+    end = reduction(
+        mlp_out,
+        grad_hidden.at[0],
+        grad_hidden.at[1, 0:3],
+        grad_hidden.at[2, 0, 0:3],
+        grad_hidden.at[2, 1, 0],
+        end_out,
+        end_ss,
+        end_rs,
+    )
+    mid[0]()
+
+    @pl.loop(0, CHUNKS)
+    def _(c):
+        grad_wait_recv(c)
+        grad_attn = mm(block(grad_recv, c), attn_out[0], NT).astype(BF)
+        for pair in range(PAIRS):
+            cut = slice(128 * pair, 128 * pair + 128)
+            piece = grad_attn[:, cut]
+            active[pair, c, :, :128] = piece
+            active[pair, c, :, 128:256] = delta_of(piece, attn_one[c, :, cut])
+
+    tile = mm(rows_of(attn_one), rows_of(grad_recv), TN)
+    mlp_out[:, :, :, 0:16, :] = shares(tile, 16)
+
+    for pair in range(PAIRS):
+        grad_key[...] = jnp.zeros((cells, 128), F32)
+        grad_value[...] = jnp.zeros((cells, 128), F32)
+
+        @pl.loop(0, CHUNKS)
+        def _(c):
+            grad_q, grad_k, grad_v = attention_back(
+                query_one[c, pair],
+                active[pair, c, :, :256],
+                lambda half: key_wide(2 * pair + half),
+                lambda half: value_wide(2 * pair + half),
+                None,
+            )
+            grad_packed[c, :, 128 * pair : 128 * pair + 128] = (grad_q * SCALE).astype(BF)
+            grad_key[...] += grad_k
+            grad_value[...] += grad_v
+
+        for c in range(CHUNKS):
+            rows = slice(BLOCK * c, BLOCK * c + BLOCK)
+            grad_packed[c, :, WIDTH + 128 * pair : WIDTH + 128 * pair + 128] = (grad_key[rows, :] * LN2).astype(BF)
+            grad_packed[c, :, 2 * WIDTH + 128 * pair : 2 * WIDTH + 128 * pair + 128] = jnp.where(
+                valid_rows(c), grad_value[rows, :], 0.0
+            ).astype(BF)
+        for part in range(3):
+            cut = slice(WIDTH * part + 128 * pair, WIDTH * part + 128 * pair + 128)
+            tile = mm(rows_of(normed_one), grad_packed[:, :, cut].reshape(cells, 128), TN)
+            mlp_out[:, :, :, 16 + 16 * part : 32 + 16 * part, 128 * pair : 128 * pair + 128] = (
+                tile.astype(BF).reshape(4, 2, GRP, 16, 128)
+            )
+        if pair < 3:
+            mid[pair + 1]()
+
+    end[0]()
+
+    @pl.loop(0, CHUNKS)
+    def _(c):
+        grad_normed = mm(grad_packed[c], attn_in[0], NT)
+        vhat, inverse = norm_stats(block(x_rows, c).astype(F32))
+        add_row(0, grad_normed * vhat)
+        add_row(3, grad_normed)
+        result = block(grad_recv, c).astype(F32) + norm_back(grad_normed, vhat, inverse, norm_gain[0:1, :])
+        normed_one[c] = result.astype(BF)
+        pltpu.make_async_copy(
+            normed_one.at[c].reshape(SWAP, PIECE, WIDTH), tokens_grad.at[:, c], out_sem.at[c]
+        ).start()
+
+    def vec_copy(source, target, index, where):
+        return pltpu.make_async_remote_copy(
+            src_ref=source,
+            dst_ref=target,
+            send_sem=vec_ss.at[index],
+            recv_sem=vec_rs.at[index],
+            device_id=where,
+            device_id_type=MESH,
+        )
+
+    vec_one = vec_copy(vectors, vec_pair, 0, {"swap": me + 1 - 2 * core})
+    vec_two = [vec_copy(vec_grp.at[grp], vec_grp.at[grp], k, {"grp": grp_peer(k)}) for k in range(1, GRP)]
+    vec_two_in = [
+        vec_copy(vec_grp.at[grp_peer(-k)], vec_grp.at[grp_peer(-k)], k, {"grp": grp_peer(-k)}) for k in range(1, GRP)
+    ]
+    vec_three = [vec_copy(vec_z.at[chip], vec_z.at[chip], 3 + k, {"swap": z_peer(k)}) for k in range(1, 4)]
+    vec_three_in = [
+        vec_copy(vec_z.at[(chip - k) % 4], vec_z.at[(chip - k) % 4], 3 + k, {"swap": z_peer(-k)}) for k in range(1, 4)
+    ]
+    vec_one.start()
+    end[1]()
+    vec_one.wait_recv()
+    vec_grp[grp] = vectors[...] + vec_pair[...]
+    for copy in vec_two:
+        copy.start()
+    end[2]()
+    for copy in vec_two_in:
+        copy.wait_recv()
+    vec_z[chip] = (vec_grp[0] + vec_grp[1]) + (vec_grp[2] + vec_grp[3])
+    for copy in vec_three:
+        copy.start()
+    end[3]()
+    for copy in vec_three_in:
+        copy.wait_recv()
+    whole = (vec_z[0] + vec_z[1]) + (vec_z[2] + vec_z[3])
+
+    def share(rows, width, step):
+        result = None
+        for index in range(WIDTH // width):
+            piece = whole[rows, index * width : index * width + width]
+            mine = step == index
+            result = jnp.where(mine, piece, 0.0 if result is None else result)
+        return result
+
+    gain_out[...] = share(slice(0, 3), 64, me)
+    offset_out[...] = share(slice(3, 6), 64, me)
+    out_bias_out[...] = share(slice(10, 11), 64, me)
+    bias_row = None
+    for index in range(4):
+        piece = share(slice(6 + index, 7 + index), 256, core)
+        bias_row = jnp.where(chip == index, piece, 0.0 if bias_row is None else bias_row)
+    hidden_bias_out[...] = bias_row
+
+    mid[4]()
+    end[4]()
+    vec_one.wait_send()
+    for copy in vec_two + vec_three:
+        copy.wait_send()
+
+    @pl.loop(0, CHUNKS)
+    def _(c):
+        own_mixed(c).wait()
+        mixed_wait_recv(c)
+        mixed_wait_send(c)
+        cot_wait_send(c)
+        grad_wait_send(c)
+        pltpu.make_async_copy(
+            normed_one.at[c].reshape(SWAP, PIECE, WIDTH), tokens_grad.at[:, c], out_sem.at[c]
+        ).wait()
+
+
+def fused_local(
+    tokens,
+    sample_counts,
+    feature_counts,
+    attn_in,
+    attn_out,
+    norm_gain,
+    norm_bias,
+    mlp_in,
+    mlp_in_bias,
+    mlp_out,
+    mlp_out_bias,
+    cotangent,
+):
+    cells = (SWAP, CHUNKS, PIECE, WIDTH)
+    blocks = (CHUNKS, SWAP, PIECE, WIDTH)
+    rows = (CHUNKS, BLOCK, WIDTH)
+    anywhere = pl.BlockSpec(memory_space=pl.ANY)
+    scalar = pl.BlockSpec(memory_space=pltpu.SMEM)
+    vector = pl.BlockSpec(memory_space=pltpu.VMEM)
+    sem = pltpu.SemaphoreType.DMA
+
+    def buffer(*shape, kind=BF):
+        return pltpu.VMEM(shape, kind)
+
+    mixed, tokens_grad, mid, end, gain, offset, hidden_bias, out_bias = pl.pallas_call(
+        fused_kernel,
+        name="layer",
+        out_shape=(
+            jax.ShapeDtypeStruct(cells, BF),
+            jax.ShapeDtypeStruct(cells, BF),
+            jax.ShapeDtypeStruct((GRP, MID_ROWS, WIDTH), BF),
+            jax.ShapeDtypeStruct((GRP, END_ROWS, WIDTH), BF),
+            jax.ShapeDtypeStruct((3, 64), F32),
+            jax.ShapeDtypeStruct((3, 64), F32),
+            jax.ShapeDtypeStruct((1, 256), F32),
+            jax.ShapeDtypeStruct((1, 64), F32),
+        ),
+        in_specs=[
+            anywhere,
+            anywhere,
+            scalar,
+            scalar,
+            anywhere,
+            anywhere,
+            vector,
+            vector,
+            anywhere,
+            vector,
+            anywhere,
+            vector,
+        ],
+        out_specs=(anywhere, anywhere, anywhere, anywhere, vector, vector, vector, vector),
+        scratch_shapes=[
+            buffer(2, WIDTH, 3 * WIDTH),
+            buffer(2, WIDTH, WIDTH),
+            buffer(WIDTH, 4 * WIDTH),
+            buffer(4, 2, GRP, END_ROWS, WIDTH),
+            buffer(*blocks),
+            buffer(*rows),
+            buffer(CHUNKS, PAIRS, BLOCK, 256),
+            buffer(HEADS, CHUNKS, BLOCK, 128),
+            buffer(HEADS, CHUNKS, BLOCK, 128),
+            buffer(2, CHUNKS, BLOCK, 128),
+            buffer(2, CHUNKS, BLOCK, 128),
+            buffer(*rows),
+            buffer(*blocks),
+            buffer(*blocks),
+            buffer(*blocks),
+            buffer(*blocks),
+            buffer(*rows),
+            buffer(*rows),
+            buffer(*rows),
+            buffer(4, *rows),
+            buffer(4, CHUNKS, GRP, END_ROWS, WIDTH),
+            buffer(CHUNKS, BLOCK, 3 * WIDTH),
+            buffer(*rows),
+            buffer(PAIRS, BLOCK, 256),
+            buffer(HEADS, BLOCK, 256),
+            buffer(HEADS, BLOCK, 256),
+            buffer(BLOCK, BLOCK, kind=F32),
+            buffer(8, WIDTH, kind=F32),
+            buffer(CHUNKS * BLOCK, 128, kind=F32),
+            buffer(CHUNKS * BLOCK, 128, kind=F32),
+            buffer(256, 128),
+            buffer(16, WIDTH, kind=F32),
+            buffer(16, WIDTH, kind=F32),
+            buffer(GRP, 16, WIDTH, kind=F32),
+            buffer(4, 16, WIDTH, kind=F32),
+            buffer(4, 2, GRP, MID_ROWS, WIDTH),
+            buffer(4, GRP, MID_ROWS, WIDTH),
+            buffer(3, 4, MID_ROWS, WIDTH),
+            buffer(3, MID_ROWS, WIDTH),
+            buffer(MID_ROWS, WIDTH),
+            sem((CHUNKS + 6,)),
+        ]
+        + [sem((CHUNKS, SWAP))] * 8
+        + [sem((CHUNKS,))]
+        + [sem((11,))] * 4
+        + [sem((7,))] * 2,
+        compiler_params=pltpu.CompilerParams(
+            collective_id=0, has_side_effects=True, vmem_limit_bytes=VMEM_LIMIT
+        ),
+    )(
+        tokens.reshape(cells),
+        cotangent.reshape(cells),
+        sample_counts,
+        feature_counts,
+        attn_in,
+        attn_out,
+        norm_gain,
+        norm_bias,
+        mlp_in,
+        mlp_in_bias.reshape(1, -1),
+        mlp_out.reshape(4, 2, GRP, END_ROWS, WIDTH),
+        mlp_out_bias.reshape(1, -1),
+    )
+
+    def columns(shares, first, count):
+        piece = shares[:, first : first + 16 * count].reshape(GRP, count, 16, WIDTH)
+        return jnp.transpose(piece, (0, 2, 1, 3)).reshape(64, count * WIDTH).astype(F32)
+
+    return (
+        mixed.reshape(tokens.shape),
+        tokens_grad.reshape(tokens.shape),
+        jnp.stack([columns(end, 16, 3), columns(mid, 128, 3)]),
+        jnp.stack([columns(end, 0, 1), columns(mid, 176, 1)]),
+        gain,
+        offset,
+        columns(mid, 0, 4),
+        hidden_bias.reshape(-1),
+        mid[:, 64:128].reshape(256, WIDTH).astype(F32),
+        out_bias.reshape(-1),
+    )
+
+
 def solution(mesh):
     placed = (
         P("grp", None, "swap", None),
@@ -238,8 +1068,17 @@
         P(),
         P("grp", None, "swap", None),
     )
+    def layer(*args):
+        tokens, mlp_in = args[0], args[7]
+        fits = (
+            (mesh.shape["swap"], mesh.shape["grp"]) == (SWAP, GRP)
+            and tokens.shape == (1, CHUNKS * BLOCK, 1, WIDTH)
+            and mlp_in.shape == (WIDTH, 4 * WIDTH)
+        )
+        return fused_local(*args) if fits else local(*args)
+
     return jax.shard_map(
-        local,
+        layer,
         mesh=mesh,
         in_specs=placed,
         out_specs=(

time: 696 us -> 214 us (0.31); the launches traced: 687 us -> 214 us
  Pallas kernels: 0 us -> 200 us
  matrix products: 188 us -> 0 us
  waiting for transfers between devices: 184 us -> 0 us
  other arithmetic: 117 us -> 2.58 us
  local copies, waits for them, and re-layouts: 122 us -> 9.24 us
  blocking collectives: 37.3 us -> 0 us
  starting transfers between devices: 21.4 us -> 0 us
  between operations: 18.1 us -> 2.04 us
    pallas_call x0 -> x1, Pallas kernels: none -> 200 us  [fused_local(): pl.pallas_call(fused_kernel, name='layer', out_shape=(jax.ShapeDtypeStruc...]
    dot_general x30 -> x0, matrix products: 188 us -> none  [the longest x6 28.2 us: weight_grad(): jnp.einsum('nd,nc->dc', left.reshape(-1, left.shape[-1]), grad_rows.resha...]
    convert_element_type x18 -> x2, other arithmetic: 71 us -> 0.92 us  [the longest x1 0.87 us: fused_local(): mid[:, 64:128].reshape(256, WIDTH).astype(F32)]
    reduce_scatter x4 -> x0, waiting for transfers between devices: 67.4 us -> none  [the longest x1 67.4 us: local(): lax.psum_scatter(stack_in, 'swap', scatter_dimension=1, tiled=True)]
    psum x1 -> x0, waiting for transfers between devices: 42.8 us -> none  [local(): lax.psum(part_in.astype(jnp.bfloat16), 'grp').astype(jnp.float32)]
    all_to_all x4 -> x0, waiting for transfers between devices: 41.6 us -> none  [the longest x1 23.2 us: local(): lax.all_to_all(grad_first, 'swap', split_axis=2, concat_axis=1, tiled=True)]
    convert_element_type x12 -> x5, local copies, waits for them, and re-layouts: 38.6 us -> 1.23 us  [columns(): jnp.transpose(piece, (0, 2, 1, 3)).reshape(64, count * WIDTH).astype(F32)]
    unnamed x154 -> x21, local copies, waits for them, and re-layouts: 38.1 us -> 5.16 us
  transfers between devices with their start and end apart: 11 -> 0, of which waited for: 6 -> 0; matrix products, arithmetic and copies ran while one was open for 33% -> 0% of each run, Pallas kernels for 0% -> 0%
where the time goes in v1:
time: 214 us
  Pallas kernels  200 us (93%)
  local copies, waits for them, and re-layouts  9.24 us (4%)
  other arithmetic  2.58 us (1%)
    pallas_call x1, Pallas kernels, fused_local(): pl.pallas_call(fused_kernel, name='layer', out_shape=(jax.ShapeDtypeStruc...  200 us
    unnamed x21, local copies, waits for them, and re-layouts  5.16 us

profile of v1, /device:TPU:0, one launch (start us, length us, event | category | flops | bytes accessed | tf_op | source)
XLA Modules:
  0.0 213.6 jit_solution(13058673853838596375)
XLA Ops:
  1.9 199.7 %layer.1 = (bf16[8,4,32,512]{3,2,1,0:T(8,128)(2,1)}, bf16[8,4,32,512]{3,2,1,0:T(8,128)(2,1)}, bf16[4,192,512]{2,1,0:T(8,128)(2,1)}, bf16[4,64,512]{2,1,0:T(8,128...) custom-call(bf16[8,4,32,512]{3,2,1,0:T(8,128)(2,1)} %bitcast.36, ...), custom_call_target="tpu_custom_call" | custom-call | tf_op jit(solution)/shard_map/layer/pallas_call | solution.py:945
  201.7 0.0 copy-start.2
  201.7 1.0 slice.19
  202.7 0.2 copy.31
  202.9 0.3 convert_element_type.79
  203.2 0.9 slice.18
  204.1 0.2 copy.32
  204.3 0.3 convert_element_type.76
  204.6 0.9 maximum_convert_fusion
  205.5 0.0 copy-done.2
  205.5 0.8 slice.20
  206.4 0.7 maximum_convert_fusion.1
  207.1 0.0 copy-start.1
  207.1 0.1 convert_bitcast_fusion
  207.2 0.3 copy.27
  207.5 0.0 copy-start
  207.5 1.0 copy.28
  208.5 0.9 bitcast_convert_fusion
  209.4 0.0 copy-done.1
  209.4 0.0 copy-start.4
  209.4 0.0 copy-start.6
  209.4 1.0 copy.41
  210.4 0.0 copy-done
  210.4 1.0 copy.42
  211.3 0.0 copy-done.4
  211.3 0.6 copy.43
  211.9 0.0 copy-done.3
  211.9 0.6 copy.44
  212.5 0.0 copy-done.5
  212.5 0.6 copy.45
  213.1 0.0 copy-done.6
  213.1 0.5 copy.46
  (4 shorter events, 0.0 us)
Async XLA Ops:
  201.7 3.8 %copy-start.2 = (bf16[4,192,512]{2,1,0:T(8,128)(2,1)S(1)}, bf16[4,192,512]{2,1,0:T(8,128)(2,1)}, u32[]{:S(2)}) copy-start(bf16[4,192,512]{2,1,0:T(8,128)(2,1)} %get-tuple-element.21) | copy-start | bytes 2359300
  207.1 2.3 %copy-start.1 = (bf16[8,4,32,512]{3,2,1,0:T(8,128)(2,1)S(1)}, bf16[8,4,32,512]{3,2,1,0:T(8,128)(2,1)}, u32[]{:S(2)}) copy-start(bf16[8,4,32,512]{3,2,1,0:T(8,128)(2,1)} %get-tuple-element.18) | copy-start | bytes 3145732
  207.5 2.8 %copy-start = (bf16[8,4,32,512]{3,2,1,0:T(8,128)(2,1)S(1)}, bf16[8,4,32,512]{3,2,1,0:T(8,128)(2,1)}, u32[]{:S(2)}) copy-start(bf16[8,4,32,512]{3,2,1,0:T(8,128)(2,1)} %get-tuple-element.19) | copy-start | bytes 3145732
  209.4 2.0 copy-start.4
  209.4 2.5 %copy-start.3 = (f32[3,64]{1,0:T(4,128)S(1)}, f32[3,64]{1,0:T(4,128)}, u32[]{:S(2)}) copy-start(f32[3,64]{1,0:T(4,128)} %get-tuple-element.43) | copy-start | bytes 2308
  209.4 3.1 %copy-start.5 = (f32[1,256]{1,0:T(1,128)S(1)}, f32[1,256]{1,0:T(1,128)}, u32[]{:S(2)}) copy-start(f32[1,256]{1,0:T(1,128)} %get-tuple-element.24) | copy-start | bytes 3076
  209.4 3.7 %copy-start.6 = (f32[1,64]{1,0:T(1,128)S(1)}, f32[1,64]{1,0:T(1,128)}, u32[]{:S(2)}) copy-start(f32[1,64]{1,0:T(1,128)} %get-tuple-element.25) | copy-start | bytes 772

commit v2 on v1

--- a/solution.py
+++ b/solution.py
@@ -242,8 +242,8 @@
 PIECE = BLOCK // SWAP
 PAIRS = 4
 WIDTH = 512
-MID_ROWS = 192
-END_ROWS = 64
+SHARE = 64
+SUMS = 4
 
 
 def mm(left, right, form=NN):
@@ -338,24 +338,24 @@
     feature_counts,
     attn_in_hbm,
     attn_out_hbm,
+    norm_gain_hbm,
+    norm_bias_hbm,
+    mlp_in_hbm,
+    mlp_in_bias_hbm,
+    mlp_out_hbm,
+    mlp_out_bias_hbm,
+    mixed,
+    tokens_grad,
+    sums,
+    small,
+    attn_in,
+    attn_out,
     norm_gain,
     norm_bias,
-    mlp_in_hbm,
+    mlp_in,
     mlp_in_bias,
-    mlp_out_hbm,
+    mlp_out,
     mlp_out_bias,
-    mixed,
-    tokens_grad,
-    mid_out,
-    end_out,
-    gain_out,
-    offset_out,
-    hidden_bias_out,
-    out_bias_out,
-    attn_in,
-    attn_out,
-    mlp_in,
-    mlp_out,
     x_rows,
     normed_one,
     query_one,
@@ -387,11 +387,11 @@
     vec_pair,
     vec_grp,
     vec_z,
-    mid_part,
-    mid_one,
-    mid_two,
-    mid_three,
-    mid_done,
+    part_sum,
+    one_sum,
+    two_sum,
+    three_sum,
+    done_sum,
     load_sem,
     first_ss,
     first_rs,
@@ -402,10 +402,8 @@
     grad_ss,
     grad_rs,
     out_sem,
-    mid_ss,
-    mid_rs,
-    end_ss,
-    end_rs,
+    sum_ss,
+    sum_rs,
     vec_ss,
     vec_rs,
 ):
@@ -430,6 +428,10 @@
         (
             (attn_in_hbm.at[0], attn_in.at[0]),
             (attn_out_hbm.at[0], attn_out.at[0]),
+            (norm_gain_hbm, norm_gain),
+            (norm_bias_hbm, norm_bias),
+            (mlp_in_bias_hbm, mlp_in_bias),
+            (mlp_out_bias_hbm, mlp_out_bias),
             (attn_in_hbm.at[1], attn_in.at[1]),
             (attn_out_hbm.at[1], attn_out.at[1]),
             (mlp_in_hbm, mlp_in),
@@ -526,7 +528,8 @@
     def block(ref, c):
         return ref[c].reshape(BLOCK, WIDTH)
 
-    loads[CHUNKS].wait()
+    for index in (0, 2, 3):
+        loads[CHUNKS + index].wait()
 
     @pl.loop(0, CHUNKS)
     def _(c):
@@ -589,7 +592,7 @@
         def _():
             cot_begin(c + 1)
 
-    for index in range(2, 6):
+    for index in range(4, 10):
         loads[CHUNKS + index].wait()
 
     def delta_of(grad, out):
@@ -649,7 +652,7 @@
             density = jnp.exp2(hidden * hidden * (-0.5 * LOG2E)) * 0.3989422804014327
             grad_hid = ((below + hidden * density) * grad_active).astype(BF)
             active[part, c] = act
-            grad_hidden[part, c] = grad_hid.reshape(GRP, END_ROWS, WIDTH)
+            grad_hidden[part, c] = grad_hid.reshape(GRP, SHARE, WIDTH)
             add_row(6 + part, grad_hid.astype(F32))
             outcome = outcome + mm(act, weight_out)
             grad_normed = grad_normed + mm(grad_hid, mlp_in[:, cut], NT)
@@ -683,47 +686,43 @@
         grad_recv[c, me] = first_recv[c, me]
         grad_start(c)
         own_mixed(c).start()
+
+    for c in range(CHUNKS):
         mixed_start(c)
 
     def rows_of(ref):
         return ref[...].reshape(cells, WIDTH)
 
-    def shares(values, rows):
-        return values.astype(BF).reshape(4, 2, GRP, rows, WIDTH)
-
-    for part in range(4):
-        cut = slice(WIDTH * part, WIDTH * part + WIDTH)
-        tile = mm(rows_of(normed_three), grad_hidden[part].reshape(cells, WIDTH), TN)
-        mid_part[:, :, :, 16 * part : 16 * part + 16, :] = shares(tile, 16)
-        tile = mm(active[part].reshape(cells, WIDTH), rows_of(cot_recv), TN)
-        mid_part[part, :, :, 64:128, :] = tile.astype(BF).reshape(2, GRP, 64, WIDTH)
-    for part in range(3):
-        cut = slice(WIDTH * part, WIDTH * part + WIDTH)
-        tile = mm(rows_of(normed_two), grad_packed[:, :, cut].reshape(cells, WIDTH), TN)
-        mid_part[:, :, :, 128 + 16 * part : 144 + 16 * part, :] = shares(tile, 16)
-    tile = mm(rows_of(attn_two), rows_of(grad_low), TN)
-    mid_part[:, :, :, 176:192, :] = shares(tile, 16)
-
-    def reduction(part, one, two, three, done, out, send, recv):
+    def shares(values):
+        return values.astype(BF).reshape(4, 2, GRP, 16, values.shape[1])
+
+    def reduction(number, part, one, two, three, done, cut):
         def remote(source, target, index, where):
             return pltpu.make_async_remote_copy(
                 src_ref=source,
                 dst_ref=target,
-                send_sem=send.at[index],
-                recv_sem=recv.at[index],
+                send_sem=sum_ss.at[number, index],
+                recv_sem=sum_rs.at[number, index],
                 device_id=where,
                 device_id_type=MESH,
             )
 
-        step_one = [remote(part.at[:, 1 - core], one, 0, {"swap": me + 1 - 2 * core})]
+        out = sums.at[min(number, SUMS - 1), grp, :, cut]
+        step_one = [
+            remote(part.at[:, 1 - core, :, :, cut], one.at[:, :, :, cut], 0, {"swap": me + 1 - 2 * core})
+        ]
         step_two = [
-            remote(one.at[:, grp_peer(k)], two.at[k - 1], k, {"grp": grp_peer(k)}) for k in range(1, GRP)
+            remote(one.at[:, grp_peer(k), :, cut], two.at[k - 1, :, :, cut], k, {"grp": grp_peer(k)})
+            for k in range(1, GRP)
         ]
         step_three = [
-            remote(one.at[(chip + k) % 4, grp], three.at[k - 1], 3 + k, {"swap": z_peer(k)}) for k in range(1, 4)
+            remote(one.at[(chip + k) % 4, grp, :, cut], three.at[k - 1, :, cut], 3 + k, {"swap": z_peer(k)})
+            for k in range(1, 4)
         ]
-        step_four = [remote(done, out.at[grp], 6 + k, {"grp": grp_peer(k)}) for k in range(1, GRP)]
-        own = pltpu.make_async_copy(done, out.at[grp], recv.at[10])
+        step_four = [
+            remote(done.at[:, cut], out, 6 + k, {"grp": grp_peer(k)}) for k in range(1, GRP)
+        ]
+        own = pltpu.make_async_copy(done.at[:, cut], out, sum_rs.at[number, 10])
 
         def begin():
             for copy in step_one:
@@ -735,7 +734,8 @@
 
             @pl.loop(0, 4)
             def _(a):
-                one[a] = (one[a].astype(F32) + part[a, core].astype(F32)).astype(BF)
+                total = one[a, :, :, cut].astype(F32) + part[a, core, :, :, cut].astype(F32)
+                one[a, :, :, cut] = total.astype(BF)
 
             for copy in step_two:
                 copy.start()
@@ -746,10 +746,10 @@
 
             @pl.loop(0, 4)
             def _(a):
-                total = one[a, grp].astype(F32)
+                total = one[a, grp, :, cut].astype(F32)
                 for k in range(3):
-                    total = total + two[k, a].astype(F32)
-                one[a, grp] = total.astype(BF)
+                    total = total + two[k, a, :, cut].astype(F32)
+                one[a, grp, :, cut] = total.astype(BF)
 
             for copy in step_three:
                 copy.start()
@@ -757,10 +757,10 @@
         def after_three():
             for copy in step_three:
                 copy.wait_recv()
-            total = one[chip, grp].astype(F32)
+            total = one[chip, grp, :, cut].astype(F32)
             for k in range(3):
-                total = total + three[k].astype(F32)
-            done[...] = total.astype(BF)
+                total = total + three[k, :, cut].astype(F32)
+            done[:, cut] = total.astype(BF)
             own.start()
             for copy in step_four:
                 copy.start()
@@ -772,67 +772,109 @@
             for copy in step_one + step_two + step_three + step_four:
                 copy.wait_send()
 
-        return begin, after_one, after_two, after_three, finish
-
-    mid = reduction(mid_part, mid_one, mid_two, mid_three, mid_done, mid_out, mid_ss, mid_rs)
-    end = reduction(
-        mlp_out,
-        grad_hidden.at[0],
-        grad_hidden.at[1, 0:3],
-        grad_hidden.at[2, 0, 0:3],
-        grad_hidden.at[2, 1, 0],
-        end_out,
-        end_ss,
-        end_rs,
-    )
-    mid[0]()
-
-    @pl.loop(0, CHUNKS)
-    def _(c):
-        grad_wait_recv(c)
-        grad_attn = mm(block(grad_recv, c), attn_out[0], NT).astype(BF)
-        for pair in range(PAIRS):
-            cut = slice(128 * pair, 128 * pair + 128)
-            piece = grad_attn[:, cut]
-            active[pair, c, :, :128] = piece
-            active[pair, c, :, 128:256] = delta_of(piece, attn_one[c, :, cut])
-
-    tile = mm(rows_of(attn_one), rows_of(grad_recv), TN)
-    mlp_out[:, :, :, 0:16, :] = shares(tile, 16)
-
-    for pair in range(PAIRS):
-        grad_key[...] = jnp.zeros((cells, 128), F32)
-        grad_value[...] = jnp.zeros((cells, 128), F32)
+        return [begin, after_one, after_two, after_three, finish]
+
+    every = slice(0, WIDTH)
+    mid = [
+        reduction(
+            number,
+            part_sum.at[number],
+            one_sum.at[number],
+            two_sum.at[number],
+            three_sum.at[number],
+            done_sum.at[number],
+            every,
+        )
+        for number in range(3)
+    ]
+    end = [
+        reduction(
+            3 + half,
+            mlp_out,
+            grad_hidden.at[0],
+            grad_hidden.at[1, 0:3],
+            grad_hidden.at[2, 0, 0:3],
+            grad_hidden.at[2, 1, 0],
+            slice(256 * half, 256 * half + 256),
+        )
+        for half in range(2)
+    ]
+
+    for part in range(4):
+        tile = mm(rows_of(normed_three), grad_hidden[part].reshape(cells, WIDTH), TN)
+        part_sum[0, :, :, :, 16 * part : 16 * part + 16, :] = shares(tile)
+    mid[0][0]()
+    for part in range(4):
+        tile = mm(active[part].reshape(cells, WIDTH), rows_of(cot_recv), TN)
+        part_sum[1, part] = tile.astype(BF).reshape(2, GRP, SHARE, WIDTH)
+    mid[1][0]()
+    mid[0][1]()
+    for part in range(3):
+        cut = slice(WIDTH * part, WIDTH * part + WIDTH)
+        tile = mm(rows_of(normed_two), grad_packed[:, :, cut].reshape(cells, WIDTH), TN)
+        part_sum[2, :, :, :, 16 * part : 16 * part + 16, :] = shares(tile)
+    tile = mm(rows_of(attn_two), rows_of(grad_low), TN)
+    part_sum[2, :, :, :, 48:64, :] = shares(tile)
+    mid[2][0]()
+    mid[1][1]()
+
+    def run(hooks, c):
+        for when, call in hooks:
+
+            @pl.when(c == when)
+            def _():
+                call()
+
+    hooks = (
+        ((0, mid[2][1]), (3, mid[0][2])),
+        ((0, mid[1][2]), (1, end[0][1]), (2, mid[0][3]), (3, mid[2][2])),
+        ((0, end[0][2]), (1, mid[1][3]), (2, end[1][1])),
+    )
+    for half in range(2):
+        pairs = (2 * half, 2 * half + 1)
+        grad_key[...] = jnp.zeros((2, cells, 128), F32)
+        grad_value[...] = jnp.zeros((2, cells, 128), F32)
 
         @pl.loop(0, CHUNKS)
         def _(c):
-            grad_q, grad_k, grad_v = attention_back(
-                query_one[c, pair],
-                active[pair, c, :, :256],
-                lambda half: key_wide(2 * pair + half),
-                lambda half: value_wide(2 * pair + half),
-                None,
-            )
-            grad_packed[c, :, 128 * pair : 128 * pair + 128] = (grad_q * SCALE).astype(BF)
-            grad_key[...] += grad_k
-            grad_value[...] += grad_v
-
-        for c in range(CHUNKS):
-            rows = slice(BLOCK * c, BLOCK * c + BLOCK)
-            grad_packed[c, :, WIDTH + 128 * pair : WIDTH + 128 * pair + 128] = (grad_key[rows, :] * LN2).astype(BF)
-            grad_packed[c, :, 2 * WIDTH + 128 * pair : 2 * WIDTH + 128 * pair + 128] = jnp.where(
-                valid_rows(c), grad_value[rows, :], 0.0
-            ).astype(BF)
+            if half == 0:
+                grad_wait_recv(c)
+                grad_attn = mm(block(grad_recv, c), attn_out[0], NT).astype(BF)
+                for pair in range(PAIRS):
+                    cut = slice(128 * pair, 128 * pair + 128)
+                    piece = grad_attn[:, cut]
+                    active[pair, c, :, :128] = piece
+                    active[pair, c, :, 128:256] = delta_of(piece, attn_one[c, :, cut])
+            for pair in pairs:
+                grad_q, grad_k, grad_v = attention_back(
+                    query_one[c, pair],
+                    active[pair, c, :, :256],
+                    lambda side: key_wide(2 * pair + side),
+                    lambda side: value_wide(2 * pair + side),
+                    None,
+                )
+                grad_packed[c, :, 128 * pair : 128 * pair + 128] = (grad_q * SCALE).astype(BF)
+                grad_key[pair % 2] += grad_k
+                grad_value[pair % 2] += grad_v
+            run(hooks[half], c)
+
+        for pair in pairs:
+            for c in range(CHUNKS):
+                rows = slice(BLOCK * c, BLOCK * c + BLOCK)
+                grad_packed[c, :, WIDTH + 128 * pair : WIDTH + 128 * pair + 128] = (
+                    grad_key[pair % 2, rows, :] * LN2
+                ).astype(BF)
+                grad_packed[c, :, 2 * WIDTH + 128 * pair : 2 * WIDTH + 128 * pair + 128] = jnp.where(
+                    valid_rows(c), grad_value[pair % 2, rows, :], 0.0
+                ).astype(BF)
+        if half == 0:
+            tile = mm(rows_of(attn_one), rows_of(grad_recv), TN)
+            mlp_out[:, :, :, 0:16, :] = shares(tile)
         for part in range(3):
-            cut = slice(WIDTH * part + 128 * pair, WIDTH * part + 128 * pair + 128)
-            tile = mm(rows_of(normed_one), grad_packed[:, :, cut].reshape(cells, 128), TN)
-            mlp_out[:, :, :, 16 + 16 * part : 32 + 16 * part, 128 * pair : 128 * pair + 128] = (
-                tile.astype(BF).reshape(4, 2, GRP, 16, 128)
-            )
-        if pair < 3:
-            mid[pair + 1]()
-
-    end[0]()
+            cut = slice(WIDTH * part + 256 * half, WIDTH * part + 256 * half + 256)
+            tile = mm(rows_of(normed_one), grad_packed[:, :, cut].reshape(cells, 256), TN)
+            mlp_out[:, :, :, 16 + 16 * part : 32 + 16 * part, 256 * half : 256 * half + 256] = shares(tile)
+        end[half][0]()
 
     @pl.loop(0, CHUNKS)
     def _(c):
@@ -845,6 +887,7 @@
         pltpu.make_async_copy(
             normed_one.at[c].reshape(SWAP, PIECE, WIDTH), tokens_grad.at[:, c], out_sem.at[c]
         ).start()
+        run(hooks[2], c)
 
     def vec_copy(source, target, index, where):
         return pltpu.make_async_remote_copy(
@@ -866,18 +909,19 @@
         vec_copy(vec_z.at[(chip - k) % 4], vec_z.at[(chip - k) % 4], 3 + k, {"swap": z_peer(-k)}) for k in range(1, 4)
     ]
     vec_one.start()
-    end[1]()
+    end[0][3]()
     vec_one.wait_recv()
     vec_grp[grp] = vectors[...] + vec_pair[...]
     for copy in vec_two:
         copy.start()
-    end[2]()
+    end[1][2]()
     for copy in vec_two_in:
         copy.wait_recv()
     vec_z[chip] = (vec_grp[0] + vec_grp[1]) + (vec_grp[2] + vec_grp[3])
     for copy in vec_three:
         copy.start()
-    end[3]()
+    mid[2][3]()
+    end[1][3]()
     for copy in vec_three_in:
         copy.wait_recv()
     whole = (vec_z[0] + vec_z[1]) + (vec_z[2] + vec_z[3])
@@ -890,17 +934,17 @@
             result = jnp.where(mine, piece, 0.0 if result is None else result)
         return result
 
-    gain_out[...] = share(slice(0, 3), 64, me)
-    offset_out[...] = share(slice(3, 6), 64, me)
-    out_bias_out[...] = share(slice(10, 11), 64, me)
+    small[0:3, 0:64] = share(slice(0, 3), 64, me)
+    small[3:6, 0:64] = share(slice(3, 6), 64, me)
     bias_row = None
     for index in range(4):
         piece = share(slice(6 + index, 7 + index), 256, core)
         bias_row = jnp.where(chip == index, piece, 0.0 if bias_row is None else bias_row)
-    hidden_bias_out[...] = bias_row
-
-    mid[4]()
-    end[4]()
+    small[6:7, :] = bias_row
+    small[7:8, 0:64] = share(slice(10, 11), 64, me)
+
+    for steps in mid + end:
+        steps[4]()
     vec_one.wait_send()
     for copy in vec_two + vec_three:
         copy.wait_send()
@@ -915,6 +959,34 @@
         pltpu.make_async_copy(
             normed_one.at[c].reshape(SWAP, PIECE, WIDTH), tokens_grad.at[:, c], out_sem.at[c]
         ).wait()
+
+
+def finish_kernel(mixed, tokens_grad, sums, small, *refs):
+    outs, row_sem = refs[:10], refs[10]
+    copies = [
+        pltpu.make_async_copy(mixed, outs[0], row_sem.at[0]),
+        pltpu.make_async_copy(tokens_grad, outs[1], row_sem.at[1]),
+    ]
+    for copy in copies:
+        copy.start()
+    for grp in range(GRP):
+        rows = slice(16 * grp, 16 * grp + 16)
+        for part in range(4):
+            cut = slice(WIDTH * part, WIDTH * part + WIDTH)
+            piece = slice(16 * part, 16 * part + 16)
+            outs[6][rows, cut] = sums[0, grp, piece].astype(F32)
+            if part < 3:
+                outs[2][1, rows, cut] = sums[2, grp, piece].astype(F32)
+                outs[2][0, rows, cut] = sums[3, grp, 16 * part + 16 : 16 * part + 32].astype(F32)
+        outs[8][SHARE * grp : SHARE * grp + SHARE] = sums[1, grp].astype(F32)
+        outs[3][1, rows] = sums[2, grp, 48:64].astype(F32)
+        outs[3][0, rows] = sums[3, grp, 0:16].astype(F32)
+    outs[4][...] = small[0:3, 0:64]
+    outs[5][...] = small[3:6, 0:64]
+    outs[7][...] = small[6:7, 0:256]
+    outs[9][...] = small[7:8, 0:64]
+    for copy in copies:
+        copy.wait()
 
 
 def fused_local(
@@ -942,39 +1014,29 @@
     def buffer(*shape, kind=BF):
         return pltpu.VMEM(shape, kind)
 
-    mixed, tokens_grad, mid, end, gain, offset, hidden_bias, out_bias = pl.pallas_call(
+    def result(shape, kind=F32):
+        return jax.ShapeDtypeStruct(shape, kind)
+
+    mixed, tokens_grad, sums, small = pl.pallas_call(
         fused_kernel,
         name="layer",
         out_shape=(
-            jax.ShapeDtypeStruct(cells, BF),
-            jax.ShapeDtypeStruct(cells, BF),
-            jax.ShapeDtypeStruct((GRP, MID_ROWS, WIDTH), BF),
-            jax.ShapeDtypeStruct((GRP, END_ROWS, WIDTH), BF),
-            jax.ShapeDtypeStruct((3, 64), F32),
-            jax.ShapeDtypeStruct((3, 64), F32),
-            jax.ShapeDtypeStruct((1, 256), F32),
-            jax.ShapeDtypeStruct((1, 64), F32),
+            result(cells, BF),
+            result(cells, BF),
+            result((SUMS, GRP, SHARE, WIDTH), BF),
+            result((8, 256)),
         ),
-        in_specs=[
-            anywhere,
-            anywhere,
-            scalar,
-            scalar,
-            anywhere,
-            anywhere,
-            vector,
-            vector,
-            anywhere,
-            vector,
-            anywhere,
-            vector,
-        ],
-        out_specs=(anywhere, anywhere, anywhere, anywhere, vector, vector, vector, vector),
+        in_specs=[anywhere, anywhere, scalar, scalar] + [anywhere] * 8,
+        out_specs=(anywhere, anywhere, anywhere, vector),
         scratch_shapes=[
             buffer(2, WIDTH, 3 * WIDTH),
             buffer(2, WIDTH, WIDTH),
+            buffer(3, WIDTH, kind=F32),
+            buffer(3, WIDTH, kind=F32),
             buffer(WIDTH, 4 * WIDTH),
-            buffer(4, 2, GRP, END_ROWS, WIDTH),
+            buffer(1, 4 * WIDTH, kind=F32),
+            buffer(4, 2, GRP, SHARE, WIDTH),
+            buffer(1, WIDTH, kind=F32),
             buffer(*blocks),
             buffer(*rows),
             buffer(CHUNKS, PAIRS, BLOCK, 256),
@@ -991,7 +1053,7 @@
             buffer(*rows),
             buffer(*rows),
             buffer(4, *rows),
-            buffer(4, CHUNKS, GRP, END_ROWS, WIDTH),
+            buffer(4, CHUNKS, GRP, SHARE, WIDTH),
             buffer(CHUNKS, BLOCK, 3 * WIDTH),
             buffer(*rows),
             buffer(PAIRS, BLOCK, 256),
@@ -999,23 +1061,23 @@
             buffer(HEADS, BLOCK, 256),
             buffer(BLOCK, BLOCK, kind=F32),
             buffer(8, WIDTH, kind=F32),
-            buffer(CHUNKS * BLOCK, 128, kind=F32),
-            buffer(CHUNKS * BLOCK, 128, kind=F32),
+            buffer(2, CHUNKS * BLOCK, 128, kind=F32),
+            buffer(2, CHUNKS * BLOCK, 128, kind=F32),
             buffer(256, 128),
             buffer(16, WIDTH, kind=F32),
             buffer(16, WIDTH, kind=F32),
             buffer(GRP, 16, WIDTH, kind=F32),
             buffer(4, 16, WIDTH, kind=F32),
-            buffer(4, 2, GRP, MID_ROWS, WIDTH),
-            buffer(4, GRP, MID_ROWS, WIDTH),
-            buffer(3, 4, MID_ROWS, WIDTH),
-            buffer(3, MID_ROWS, WIDTH),
-            buffer(MID_ROWS, WIDTH),
-            sem((CHUNKS + 6,)),
+            buffer(3, 4, 2, GRP, SHARE, WIDTH),
+            buffer(3, 4, GRP, SHARE, WIDTH),
+            buffer(3, 3, 4, SHARE, WIDTH),
+            buffer(3, 3, SHARE, WIDTH),
+            buffer(3, SHARE, WIDTH),
+            sem((CHUNKS + 10,)),
         ]
         + [sem((CHUNKS, SWAP))] * 8
         + [sem((CHUNKS,))]
-        + [sem((11,))] * 4
+        + [sem((5, 11))] * 2
         + [sem((7,))] * 2,
         compiler_params=pltpu.CompilerParams(
             collective_id=0, has_side_effects=True, vmem_limit_bytes=VMEM_LIMIT
@@ -1031,25 +1093,37 @@
         norm_bias,
         mlp_in,
         mlp_in_bias.reshape(1, -1),
-        mlp_out.reshape(4, 2, GRP, END_ROWS, WIDTH),
+        mlp_out.reshape(4, 2, GRP, SHARE, WIDTH),
         mlp_out_bias.reshape(1, -1),
     )
-
-    def columns(shares, first, count):
-        piece = shares[:, first : first + 16 * count].reshape(GRP, count, 16, WIDTH)
-        return jnp.transpose(piece, (0, 2, 1, 3)).reshape(64, count * WIDTH).astype(F32)
-
+    shapes = (
+        result(cells, BF),
+        result(cells, BF),
+        result((2, 64, 3 * WIDTH)),
+        result((2, 64, WIDTH)),
+        result((3, 64)),
+        result((3, 64)),
+        result((64, 4 * WIDTH)),
+        result((1, 256)),
+        result((256, WIDTH)),
+        result((1, 64)),
+    )
+    outs = pl.pallas_call(
+        finish_kernel,
+        name="results",
+        out_shape=shapes,
+        in_specs=[anywhere, anywhere, vector, vector],
+        out_specs=(anywhere, anywhere) + (vector,) * 8,
+        scratch_shapes=[sem((2,))],
+        compiler_params=pltpu.CompilerParams(vmem_limit_bytes=16 * 1024 * 1024),
+    )(mixed, tokens_grad, sums, small)
     return (
-        mixed.reshape(tokens.shape),
-        tokens_grad.reshape(tokens.shape),
-        jnp.stack([columns(end, 16, 3), columns(mid, 128, 3)]),
-        jnp.stack([columns(end, 0, 1), columns(mid, 176, 1)]),
-        gain,
-        offset,
-        columns(mid, 0, 4),
-        hidden_bias.reshape(-1),
-        mid[:, 64:128].reshape(256, WIDTH).astype(F32),
-        out_bias.reshape(-1),
+        outs[0].reshape(tokens.shape),
+        outs[1].reshape(tokens.shape),
+        *outs[2:7],
+        outs[7].reshape(-1),
+        outs[8],
+        outs[9].reshape(-1),
     )
 
 

time: 214 us -> 154 us (0.72)
  Pallas kernels: 200 us -> 147 us
  local copies, waits for them, and re-layouts: 9.24 us -> 4.36 us
  other arithmetic: 2.58 us -> 0 us
    pallas_call x1 -> x2, Pallas kernels: 200 us -> 147 us  [the longest x1 144 us: fused_local(): pl.pallas_call(fused_kernel, name='layer', out_shape=(result(cells, BF),...]
    slice x5 -> x0, local copies, waits for them, and re-layouts: 2.85 us -> none  [the longest x4 2.82 us: columns(): piece = shares[:, first:first + 16 * count].reshape(GRP, count, 16, WIDTH)]
    unnamed x21 -> x8, local copies, waits for them, and re-layouts: 5.16 us -> 4.36 us
where the time goes in v2:
time: 154 us
  Pallas kernels  147 us (95%)
  local copies, waits for them, and re-layouts  4.36 us (3%)
  between operations  2.14 us (1%)
    pallas_call x1, Pallas kernels, fused_local(): pl.pallas_call(fused_kernel, name='layer', out_shape=(result(cells, BF),...  144 us
    unnamed x8, local copies, waits for them, and re-layouts  4.36 us

profile of v2, /device:TPU:0, one launch (start us, length us, event | category | flops | bytes accessed | tf_op | source)
XLA Modules:
  0.0 153.6 jit_solution(16367204424136308273)
XLA Ops:
  1.9 144.4 %layer.1 = (bf16[8,4,32,512]{3,2,1,0:T(8,128)(2,1)}, bf16[8,4,32,512]{3,2,1,0:T(8,128)(2,1)}, bf16[4,4,64,512]{3,2,1,0:T(8,128)(2,1)}, f32[8,256]{1,0:T(8,128)}) custom-call(bf16[8,4,32,512]{3,2,1,0:T(8,128)(2,1)} %bitcast.10, bf16[8,4,32,512]{3,2,1,0:T(8,128)(2,1)} %bitcast.11, s32[1]{0:T(128)S(6)} %copy.22.sample_counts, s32[1]{0:T(128)S(6)} %copy.23.feature_counts, ...), custom_call_target="tpu_custom_call" | custom-call | tf_op jit(solution)/shard_map/layer/pallas_call | solution.py:1020
  146.4 0.0 copy-start
  146.4 1.2 copy-done
  147.6 0.0 copy-start.1
  147.6 1.2 copy-done.1
  148.8 0.0 copy-start.2
  148.8 1.2 copy-done.2
  150.0 0.0 copy-start.3
  150.0 0.7 copy-done.3
  150.7 2.7 %results.1 = (bf16[8,4,32,512]{3,2,1,0:T(8,128)(2,1)}, bf16[8,4,32,512]{3,2,1,0:T(8,128)(2,1)}, f32[2,64,1536]{2,1,0:T(8,128)}, f32[2,64,512]{2,1,0:T(8,128)}, f...) custom-call(bf16[8,4,32,512]{3,2,1,0:T(8,128)(2,1)S(1)} %copy-done, ...), custom_call_target="tpu_custom_call" | custom-call | tf_op jit(solution)/shard_map/results/pallas_call | solution.py:1111
Async XLA Ops:
  146.4 1.2 copy-start
  147.6 1.2 copy-start.1
  148.8 1.2 copy-start.2
  150.0 0.7 copy-start.3

commit v3 on v2

--- a/solution.py
+++ b/solution.py
@@ -411,6 +411,10 @@
     me = lax.axis_index("swap")
     chip = me // 2
     core = me % 2
+    col = grp % 2
+    row = grp // 2
+    odd = chip % 2
+    upper = chip // 2
     samples = sample_counts[0]
     features = feature_counts[0]
 
@@ -498,6 +502,7 @@
         cot_start(c)
 
     cot_begin(0)
+    cot_begin(1)
 
     vectors[...] = jnp.zeros((16, WIDTH), F32)
     low_half = lax.broadcasted_iota(jnp.int32, (CHUNKS, BLOCK, 128), 2) < 64
@@ -588,9 +593,161 @@
         first_recv[c, me] = first_send[c, me]
         first_start(c)
 
-        @pl.when(c < CHUNKS - 1)
+        @pl.when(c == 1)
         def _():
-            cot_begin(c + 1)
+            cot_begin(2)
+
+        @pl.when(c == 3)
+        def _():
+            cot_begin(3)
+
+    def reduction(number, part, one, two, three, done, cut):
+        def remote(source, target, index, where):
+            return pltpu.make_async_remote_copy(
+                src_ref=source,
+                dst_ref=target,
+                send_sem=sum_ss.at[number, index],
+                recv_sem=sum_rs.at[number, index],
+                device_id=where,
+                device_id_type=MESH,
+            )
+
+        beside = {"grp": grp + 1 - 2 * col}
+        above = {"grp": grp + 2 - 4 * row}
+        out = sums.at[min(number, SUMS - 1), grp, :, cut]
+        step_one = [
+            remote(part.at[:, 1 - core, :, :, :, cut], one.at[:, :, :, :, cut], 0, {"swap": me + 1 - 2 * core})
+        ]
+        step_two = [
+            remote(one.at[0:2, :, 1 - col, :, cut], two.at[0, :, :, :, cut], 1, beside),
+            remote(one.at[2:4, 1 - row, :, :, cut], two.at[1, :, :, :, cut], 2, above),
+        ]
+        step_three = [
+            remote(one.at[0:2, 1 - row, col, :, cut], two.at[2, 0, :, :, cut], 3, above),
+            remote(one.at[2:4, row, 1 - col, :, cut], two.at[2, 1, :, :, cut], 4, beside),
+        ]
+        step_four = [
+            remote(one.at[2 * k + 1 - odd, row, col, :, cut], three.at[k, :, cut], 5 + k, {"swap": me + 2 - 4 * odd})
+            for k in range(2)
+        ]
+        step_five = [
+            remote(
+                one.at[2 - 2 * upper + odd, row, col, :, cut], three.at[2, :, cut], 7, {"swap": me + 4 - 8 * upper}
+            )
+        ]
+        step_six = [remote(done.at[:, cut], out, 7 + k, {"grp": grp_peer(k)}) for k in range(1, GRP)]
+        own = pltpu.make_async_copy(done.at[:, cut], out, sum_rs.at[number, 11])
+
+        def begin():
+            for copy in step_one:
+                copy.start()
+
+        def after_one():
+            for copy in step_one:
+                copy.wait_recv()
+
+            @pl.loop(0, 4)
+            def _(a):
+                total = one[a, :, :, :, cut].astype(F32) + part[a, core, :, :, :, cut].astype(F32)
+                one[a, :, :, :, cut] = total.astype(BF)
+
+            for copy in step_two:
+                copy.start()
+
+        def after_two():
+            for copy in step_two:
+                copy.wait_recv()
+            for a in range(2):
+                total = one[a, :, col, :, cut].astype(F32) + two[0, a, :, :, cut].astype(F32)
+                one[a, :, col, :, cut] = total.astype(BF)
+                total = one[2 + a, row, :, :, cut].astype(F32) + two[1, a, :, :, cut].astype(F32)
+                one[2 + a, row, :, :, cut] = total.astype(BF)
+            for copy in step_three:
+                copy.start()
+
+        def after_three():
+            for copy in step_three:
+                copy.wait_recv()
+            for a in range(4):
+                total = one[a, row, col, :, cut].astype(F32) + two[2, a // 2, a % 2, :, cut].astype(F32)
+                one[a, row, col, :, cut] = total.astype(BF)
+            for copy in step_four:
+                copy.start()
+
+        def after_four():
+            for copy in step_four:
+                copy.wait_recv()
+            for k in range(2):
+                total = one[2 * k + odd, row, col, :, cut].astype(F32) + three[k, :, cut].astype(F32)
+                one[2 * k + odd, row, col, :, cut] = total.astype(BF)
+            for copy in step_five:
+                copy.start()
+
+        def after_five():
+            for copy in step_five:
+                copy.wait_recv()
+            total = one[chip, row, col, :, cut].astype(F32) + three[2, :, cut].astype(F32)
+            done[:, cut] = total.astype(BF)
+            own.start()
+            for copy in step_six:
+                copy.start()
+
+        def finish():
+            own.wait()
+            for copy in step_six:
+                copy.wait_recv()
+            for copy in step_one + step_two + step_three + step_four + step_five + step_six:
+                copy.wait_send()
+
+        return [begin, after_one, after_two, after_three, after_four, after_five, finish]
+
+    every = slice(0, WIDTH)
+    mid = [
+        reduction(
+            number,
+            part_sum.at[number],
+            one_sum.at[number],
+            two_sum.at[number],
+            three_sum.at[number],
+            done_sum.at[number],
+            every,
+        )
+        for number in range(3)
+    ]
+    end = [
+        reduction(
+            3 + half,
+            mlp_out,
+            grad_hidden.at[0],
+            grad_hidden.at[1, 0:3],
+            grad_hidden.at[2, 0:3, 0, 0],
+            grad_hidden.at[3, 0, 0, 0],
+            slice(256 * half, 256 * half + 256),
+        )
+        for half in range(2)
+    ]
+
+    def rows_of(ref):
+        return ref[...].reshape(cells, WIDTH)
+
+    def shares(values):
+        return values.astype(BF).reshape(4, 2, 2, 2, 16, values.shape[1])
+
+    def put_shares(number, piece, tile):
+        part_sum[number, :, :, :, :, 16 * piece : 16 * piece + 16, :] = shares(tile)
+
+    def grads_in(part):
+        put_shares(0, part, mm(rows_of(normed_three), grad_hidden[part].reshape(cells, WIDTH), TN))
+
+    def grads_out(part):
+        tile = mm(active[part].reshape(cells, WIDTH), rows_of(cot_recv), TN)
+        part_sum[1, part] = tile.astype(BF).reshape(2, 2, 2, SHARE, WIDTH)
+
+    def wide_grads(part):
+        cut = slice(WIDTH * part, WIDTH * part + WIDTH)
+        put_shares(2, part, mm(rows_of(normed_two), grad_packed[:, :, cut].reshape(cells, WIDTH), TN))
+        if part == 2:
+            put_shares(2, 3, mm(rows_of(attn_two), rows_of(grad_low), TN))
 
     for index in range(4, 10):
         loads[CHUNKS + index].wait()
@@ -604,6 +761,11 @@
     @pl.loop(0, CHUNKS)
     def _(c):
         first_wait_recv(c)
+
+        @pl.when(c == 3)
+        def _():
+            grad_start(1)
+
         resid_one = block(first_recv, c).astype(F32)
         vhat_two, inverse_two = norm_stats(resid_one)
         normed = (vhat_two * norm_gain[1:2, :] + norm_bias[1:2, :]).astype(BF)
@@ -640,6 +802,16 @@
         cot_low = block(cot_recv, c)
         cot = cot_low.astype(F32)
         add_row(10, cot)
+
+        @pl.when(c == 2)
+        def _():
+            grad_start(0)
+
+
+        @pl.when(c == 3)
+        def _():
+            grad_start(2)
+
         outcome = second + mlp_out_bias[...]
         grad_normed = jnp.zeros((BLOCK, WIDTH), F32)
         for part in range(4):
@@ -652,10 +824,20 @@
             density = jnp.exp2(hidden * hidden * (-0.5 * LOG2E)) * 0.3989422804014327
             grad_hid = ((below + hidden * density) * grad_active).astype(BF)
             active[part, c] = act
-            grad_hidden[part, c] = grad_hid.reshape(GRP, SHARE, WIDTH)
+            grad_hidden[part, c] = grad_hid.reshape(2, 2, SHARE, WIDTH)
             add_row(6 + part, grad_hid.astype(F32))
             outcome = outcome + mm(act, weight_out)
             grad_normed = grad_normed + mm(grad_hid, mlp_in[:, cut], NT)
+
+        @pl.when(c == CHUNKS - 1)
+        def _():
+            for part in range(4):
+                grads_in(part)
+            mid[0][0]()
+            for part in range(4):
+                grads_out(part)
+            mid[1][0]()
+
         first_wait_send(c)
         first_send[c] = outcome.astype(BF).reshape(SWAP, PIECE, WIDTH)
         add_row(2, grad_normed * vhat_three)
@@ -684,137 +866,16 @@
         grad_first = grad_second + norm_back(grad_normed, vhat_two, inverse_two, norm_gain[1:2, :])
         first_recv[c] = grad_first.astype(BF).reshape(SWAP, PIECE, WIDTH)
         grad_recv[c, me] = first_recv[c, me]
-        grad_start(c)
         own_mixed(c).start()
 
-    for c in range(CHUNKS):
-        mixed_start(c)
-
-    def rows_of(ref):
-        return ref[...].reshape(cells, WIDTH)
-
-    def shares(values):
-        return values.astype(BF).reshape(4, 2, GRP, 16, values.shape[1])
-
-    def reduction(number, part, one, two, three, done, cut):
-        def remote(source, target, index, where):
-            return pltpu.make_async_remote_copy(
-                src_ref=source,
-                dst_ref=target,
-                send_sem=sum_ss.at[number, index],
-                recv_sem=sum_rs.at[number, index],
-                device_id=where,
-                device_id_type=MESH,
-            )
-
-        out = sums.at[min(number, SUMS - 1), grp, :, cut]
-        step_one = [
-            remote(part.at[:, 1 - core, :, :, cut], one.at[:, :, :, cut], 0, {"swap": me + 1 - 2 * core})
-        ]
-        step_two = [
-            remote(one.at[:, grp_peer(k), :, cut], two.at[k - 1, :, :, cut], k, {"grp": grp_peer(k)})
-            for k in range(1, GRP)
-        ]
-        step_three = [
-            remote(one.at[(chip + k) % 4, grp, :, cut], three.at[k - 1, :, cut], 3 + k, {"swap": z_peer(k)})
-            for k in range(1, 4)
-        ]
-        step_four = [
-            remote(done.at[:, cut], out, 6 + k, {"grp": grp_peer(k)}) for k in range(1, GRP)
-        ]
-        own = pltpu.make_async_copy(done.at[:, cut], out, sum_rs.at[number, 10])
-
-        def begin():
-            for copy in step_one:
-                copy.start()
-
-        def after_one():
-            for copy in step_one:
-                copy.wait_recv()
-
-            @pl.loop(0, 4)
-            def _(a):
-                total = one[a, :, :, cut].astype(F32) + part[a, core, :, :, cut].astype(F32)
-                one[a, :, :, cut] = total.astype(BF)
-
-            for copy in step_two:
-                copy.start()
-
-        def after_two():
-            for copy in step_two:
-                copy.wait_recv()
-
-            @pl.loop(0, 4)
-            def _(a):
-                total = one[a, grp, :, cut].astype(F32)
-                for k in range(3):
-                    total = total + two[k, a, :, cut].astype(F32)
-                one[a, grp, :, cut] = total.astype(BF)
-
-            for copy in step_three:
-                copy.start()
-
-        def after_three():
-            for copy in step_three:
-                copy.wait_recv()
-            total = one[chip, grp, :, cut].astype(F32)
-            for k in range(3):
-                total = total + three[k, :, cut].astype(F32)
-            done[:, cut] = total.astype(BF)
-            own.start()
-            for copy in step_four:
-                copy.start()
-
-        def finish():
-            own.wait()
-            for copy in step_four:
-                copy.wait_recv()
-            for copy in step_one + step_two + step_three + step_four:
-                copy.wait_send()
-
-        return [begin, after_one, after_two, after_three, finish]
-
-    every = slice(0, WIDTH)
-    mid = [
-        reduction(
-            number,
-            part_sum.at[number],
-            one_sum.at[number],
-            two_sum.at[number],
-            three_sum.at[number],
-            done_sum.at[number],
-            every,
-        )
-        for number in range(3)
-    ]
-    end = [
-        reduction(
-            3 + half,
-            mlp_out,
-            grad_hidden.at[0],
-            grad_hidden.at[1, 0:3],
-            grad_hidden.at[2, 0, 0:3],
-            grad_hidden.at[2, 1, 0],
-            slice(256 * half, 256 * half + 256),
-        )
-        for half in range(2)
-    ]
-
-    for part in range(4):
-        tile = mm(rows_of(normed_three), grad_hidden[part].reshape(cells, WIDTH), TN)
-        part_sum[0, :, :, :, 16 * part : 16 * part + 16, :] = shares(tile)
-    mid[0][0]()
-    for part in range(4):
-        tile = mm(active[part].reshape(cells, WIDTH), rows_of(cot_recv), TN)
-        part_sum[1, part] = tile.astype(BF).reshape(2, GRP, SHARE, WIDTH)
-    mid[1][0]()
+        @pl.when(c == CHUNKS - 1)
+        def _():
+            grad_start(c)
+
     mid[0][1]()
+
     for part in range(3):
-        cut = slice(WIDTH * part, WIDTH * part + WIDTH)
-        tile = mm(rows_of(normed_two), grad_packed[:, :, cut].reshape(cells, WIDTH), TN)
-        part_sum[2, :, :, :, 16 * part : 16 * part + 16, :] = shares(tile)
-    tile = mm(rows_of(attn_two), rows_of(grad_low), TN)
-    part_sum[2, :, :, :, 48:64, :] = shares(tile)
+        wide_grads(part)
     mid[2][0]()
     mid[1][1]()
 
@@ -826,9 +887,11 @@
                 call()
 
     hooks = (
-        ((0, mid[2][1]), (3, mid[0][2])),
-        ((0, mid[1][2]), (1, end[0][1]), (2, mid[0][3]), (3, mid[2][2])),
-        ((0, end[0][2]), (1, mid[1][3]), (2, end[1][1])),
+        (),
+        ((0, mid[2][1]), (2, mid[0][2]), (3, mid[1][2]), ),
+        (),
+        ((0, mid[2][2]), (1, mid[0][3]), (1, end[0][1]), (2, mid[1][3]), (3, mid[0][4]), (3, mid[2][3]), (3, end[0][2]), ),
+        ((0, mid[1][4]), (0, end[1][1]), (1, mid[0][5]), (1, mid[2][4]), (2, end[0][3]), (2, end[1][2]), (3, mid[1][5]), ),
     )
     for half in range(2):
         pairs = (2 * half, 2 * half + 1)
@@ -839,6 +902,7 @@
         def _(c):
             if half == 0:
                 grad_wait_recv(c)
+                mixed_start(c)
                 grad_attn = mm(block(grad_recv, c), attn_out[0], NT).astype(BF)
                 for pair in range(PAIRS):
                     cut = slice(128 * pair, 128 * pair + 128)
@@ -856,7 +920,7 @@
                 grad_packed[c, :, 128 * pair : 128 * pair + 128] = (grad_q * SCALE).astype(BF)
                 grad_key[pair % 2] += grad_k
                 grad_value[pair % 2] += grad_v
-            run(hooks[half], c)
+                run(hooks[pair], c)
 
         for pair in pairs:
             for c in range(CHUNKS):
@@ -868,12 +932,12 @@
                     valid_rows(c), grad_value[pair % 2, rows, :], 0.0
                 ).astype(BF)
         if half == 0:
-            tile = mm(rows_of(attn_one), rows_of(grad_recv), TN)
-            mlp_out[:, :, :, 0:16, :] = shares(tile)
+            grad_rows = grad_recv[...].reshape(cells, WIDTH)
+            mlp_out[:, :, :, :, 0:16, :] = shares(mm(rows_of(attn_one), grad_rows, TN))
         for part in range(3):
             cut = slice(WIDTH * part + 256 * half, WIDTH * part + 256 * half + 256)
             tile = mm(rows_of(normed_one), grad_packed[:, :, cut].reshape(cells, 256), TN)
-            mlp_out[:, :, :, 16 + 16 * part : 32 + 16 * part, 256 * half : 256 * half + 256] = shares(tile)
+            mlp_out[:, :, :, :, 16 + 16 * part : 32 + 16 * part, 256 * half : 256 * half + 256] = shares(tile)
         end[half][0]()
 
     @pl.loop(0, CHUNKS)
@@ -887,7 +951,7 @@
         pltpu.make_async_copy(
             normed_one.at[c].reshape(SWAP, PIECE, WIDTH), tokens_grad.at[:, c], out_sem.at[c]
         ).start()
-        run(hooks[2], c)
+        run(hooks[4], c)
 
     def vec_copy(source, target, index, where):
         return pltpu.make_async_remote_copy(
@@ -909,19 +973,21 @@
         vec_copy(vec_z.at[(chip - k) % 4], vec_z.at[(chip - k) % 4], 3 + k, {"swap": z_peer(-k)}) for k in range(1, 4)
     ]
     vec_one.start()
-    end[0][3]()
+    mid[2][5]()
+    end[0][4]()
+    end[1][3]()
     vec_one.wait_recv()
     vec_grp[grp] = vectors[...] + vec_pair[...]
     for copy in vec_two:
         copy.start()
-    end[1][2]()
+    end[0][5]()
+    end[1][4]()
     for copy in vec_two_in:
         copy.wait_recv()
     vec_z[chip] = (vec_grp[0] + vec_grp[1]) + (vec_grp[2] + vec_grp[3])
     for copy in vec_three:
         copy.start()
-    mid[2][3]()
-    end[1][3]()
+    end[1][5]()
     for copy in vec_three_in:
         copy.wait_recv()
     whole = (vec_z[0] + vec_z[1]) + (vec_z[2] + vec_z[3])
@@ -944,7 +1010,7 @@
     small[7:8, 0:64] = share(slice(10, 11), 64, me)
 
     for steps in mid + end:
-        steps[4]()
+        steps[6]()
     vec_one.wait_send()
     for copy in vec_two + vec_three:
         copy.wait_send()
@@ -961,14 +1027,24 @@
         ).wait()
 
 
-def finish_kernel(mixed, tokens_grad, sums, small, *refs):
-    outs, row_sem = refs[:10], refs[10]
-    copies = [
-        pltpu.make_async_copy(mixed, outs[0], row_sem.at[0]),
-        pltpu.make_async_copy(tokens_grad, outs[1], row_sem.at[1]),
-    ]
-    for copy in copies:
+def finish_kernel(mixed, tokens_grad, sums_hbm, small_hbm, *refs):
+    outs, (sums, small, held, sem) = refs[:10], refs[10:]
+    loads = [pltpu.make_async_copy(sums_hbm.at[k], sums.at[k], sem.at[k]) for k in range(SUMS)]
+    loads.append(pltpu.make_async_copy(small_hbm, small, sem.at[SUMS]))
+    cells_in, cells_out = [], []
+    for index, source in enumerate((mixed, tokens_grad)):
+        for half in range(2):
+            part = slice(4 * half, 4 * half + 4)
+            place = SUMS + 1 + 2 * index + half
+            cells_in.append(pltpu.make_async_copy(source.at[part], held.at[index, part], sem.at[place]))
+            cells_out.append(pltpu.make_async_copy(held.at[index, part], outs[index].at[part], sem.at[place + 4]))
+    for copy in cells_in + loads:
         copy.start()
+    for before, after in zip(cells_in, cells_out):
+        before.wait()
+        after.start()
+    for copy in loads:
+        copy.wait()
     for grp in range(GRP):
         rows = slice(16 * grp, 16 * grp + 16)
         for part in range(4):
@@ -985,7 +1061,7 @@
     outs[5][...] = small[3:6, 0:64]
     outs[7][...] = small[6:7, 0:256]
     outs[9][...] = small[7:8, 0:64]
-    for copy in copies:
+    for copy in cells_out:
         copy.wait()
 
 
@@ -1035,7 +1111,7 @@
             buffer(3, WIDTH, kind=F32),
             buffer(WIDTH, 4 * WIDTH),
             buffer(1, 4 * WIDTH, kind=F32),
-            buffer(4, 2, GRP, SHARE, WIDTH),
+            buffer(4, 2, 2, 2, SHARE, WIDTH),
             buffer(1, WIDTH, kind=F32),
             buffer(*blocks),
             buffer(*rows),
@@ -1053,7 +1129,7 @@
             buffer(*rows),
             buffer(*rows),
             buffer(4, *rows),
-            buffer(4, CHUNKS, GRP, SHARE, WIDTH),
+            buffer(4, CHUNKS, 2, 2, SHARE, WIDTH),
             buffer(CHUNKS, BLOCK, 3 * WIDTH),
             buffer(*rows),
             buffer(PAIRS, BLOCK, 256),
@@ -1068,16 +1144,16 @@
             buffer(16, WIDTH, kind=F32),
             buffer(GRP, 16, WIDTH, kind=F32),
             buffer(4, 16, WIDTH, kind=F32),
-            buffer(3, 4, 2, GRP, SHARE, WIDTH),
-            buffer(3, 4, GRP, SHARE, WIDTH),
-            buffer(3, 3, 4, SHARE, WIDTH),
+            buffer(3, 4, 2, 2, 2, SHARE, WIDTH),
+            buffer(3, 4, 2, 2, SHARE, WIDTH),
+            buffer(3, 3, 2, 2, SHARE, WIDTH),
             buffer(3, 3, SHARE, WIDTH),
             buffer(3, SHARE, WIDTH),
             sem((CHUNKS + 10,)),
         ]
         + [sem((CHUNKS, SWAP))] * 8
         + [sem((CHUNKS,))]
-        + [sem((5, 11))] * 2
+        + [sem((5, 12))] * 2
         + [sem((7,))] * 2,
         compiler_params=pltpu.CompilerParams(
             collective_id=0, has_side_effects=True, vmem_limit_bytes=VMEM_LIMIT
@@ -1093,7 +1169,7 @@
         norm_bias,
         mlp_in,
         mlp_in_bias.reshape(1, -1),
-        mlp_out.reshape(4, 2, GRP, SHARE, WIDTH),
+        mlp_out.reshape(4, 2, 2, 2, SHARE, WIDTH),
         mlp_out_bias.reshape(1, -1),
     )
     shapes = (
@@ -1112,10 +1188,15 @@
         finish_kernel,
         name="results",
         out_shape=shapes,
-        in_specs=[anywhere, anywhere, vector, vector],
+        in_specs=[anywhere] * 4,
         out_specs=(anywhere, anywhere) + (vector,) * 8,
-        scratch_shapes=[sem((2,))],
-        compiler_params=pltpu.CompilerParams(vmem_limit_bytes=16 * 1024 * 1024),
+        scratch_shapes=[
+            buffer(SUMS, GRP, SHARE, WIDTH),
+            buffer(8, 256, kind=F32),
+            buffer(2, *cells),
+            sem((SUMS + 9,)),
+        ],
+        compiler_params=pltpu.CompilerParams(vmem_limit_bytes=VMEM_LIMIT),
     )(mixed, tokens_grad, sums, small)
     return (
         outs[0].reshape(tokens.shape),

time: 154 us -> 141 us (0.916)
  Pallas kernels: 147 us -> 139 us
  local copies, waits for them, and re-layouts: 4.36 us -> 0 us
    pallas_call x1, Pallas kernels: 144 us -> 135 us  [fused_local(): pl.pallas_call(fused_kernel, name='layer', out_shape=(result(cells, BF),...]
    unnamed x8 -> x0, local copies, waits for them, and re-layouts: 4.36 us -> none
where the time goes in v3:
time: 141 us
  Pallas kernels  139 us (99%)
  between operations  2.15 us (2%)
    pallas_call x1, Pallas kernels, fused_local(): pl.pallas_call(fused_kernel, name='layer', out_shape=(result(cells, BF),...  135 us
    pallas_call x1, Pallas kernels, fused_local(): pl.pallas_call(finish_kernel, name='results', out_shape=shapes, in_specs=...  3.79 us

profile of v3, /device:TPU:0, one launch (start us, length us, event | category | flops | bytes accessed | tf_op | source)
XLA Modules:
  0.0 140.7 jit_solution(5608399015667704124)
XLA Ops:
  1.9 134.7 %layer.1 = (bf16[8,4,32,512]{3,2,1,0:T(8,128)(2,1)}, bf16[8,4,32,512]{3,2,1,0:T(8,128)(2,1)}, bf16[4,4,64,512]{3,2,1,0:T(8,128)(2,1)}, f32[8,256]{1,0:T(8,128)}) custom-call(bf16[8,4,32,512]{3,2,1,0:T(8,128)(2,1)} %bitcast.10, bf16[8,4,32,512]{3,2,1,0:T(8,128)(2,1)} %bitcast.11, s32[1]{0:T(128)S(6)} %copy.22.sample_counts, s32[1]{0:T(128)S(6)} %copy.23.feature_counts, ...), custom_call_target="tpu_custom_call" | custom-call | tf_op jit(solution)/shard_map/layer/pallas_call | solution.py:1096
  136.7 3.8 %results.1 = (bf16[8,4,32,512]{3,2,1,0:T(8,128)(2,1)}, bf16[8,4,32,512]{3,2,1,0:T(8,128)(2,1)}, f32[2,64,1536]{2,1,0:T(8,128)}, f32[2,64,512]{2,1,0:T(8,128)}, f...) custom-call(bf16[8,4,32,512]{3,2,1,0:T(8,128)(2,1)} %get-tuple-eleme, ...), custom_call_target="tpu_custom_call" | custom-call | tf_op jit(solution)/shard_map/results/pallas_call | solution.py:1187

commit v4 on v3

--- a/solution.py
+++ b/solution.py
@@ -401,6 +401,7 @@
     mixed_rs,
     grad_ss,
     grad_rs,
+    own_sem,
     out_sem,
     sum_ss,
     sum_rs,
@@ -453,28 +454,28 @@
         pl.semaphore_signal(barrier, inc=1, device_id={"grp": grp_peer(k)}, device_id_type=MESH)
     pl.semaphore_wait(barrier, SWAP - 1 + GRP - 1)
 
+    others = slice(0, SWAP - 1)
+
     def exchange(source, target, send, recv):
-        def copy(c, d, peer):
+        def copy(c, d, come, go):
             return pltpu.make_async_remote_copy(
-                src_ref=source(c, d),
-                dst_ref=target(c, peer),
-                send_sem=send.at[c, d],
-                recv_sem=recv.at[c, peer],
+                src_ref=source(c, go),
+                dst_ref=target(c, come),
+                send_sem=send.at[c],
+                recv_sem=recv.at[c],
                 device_id={"swap": d},
                 device_id_type=MESH,
             )
 
         def start(c):
             for k in range(1, SWAP):
-                copy(c, swap_peer(k), me).start()
+                copy(c, swap_peer(k), me, swap_peer(k)).start()
 
         def wait_send(c):
-            for k in range(1, SWAP):
-                copy(c, swap_peer(k), me).wait_send()
+            copy(c, swap_peer(1), others, others).wait_send()
 
         def wait_recv(c):
-            for k in range(1, SWAP):
-                copy(c, swap_peer(k), swap_peer(k)).wait_recv()
+            copy(c, swap_peer(1), others, others).wait_recv()
 
         return start, wait_send, wait_recv
 
@@ -492,17 +493,16 @@
     )
 
     def own_cot(c):
-        return pltpu.make_async_copy(cotangent.at[me, c], cot_recv.at[c, me], cot_rs.at[c, me])
+        return pltpu.make_async_copy(cotangent.at[me, c], cot_recv.at[c, me], own_sem.at[0, c])
 
     def own_mixed(c):
-        return pltpu.make_async_copy(first_send.at[c, me], mixed.at[me, c], mixed_rs.at[c, me])
+        return pltpu.make_async_copy(first_send.at[c, me], mixed.at[me, c], own_sem.at[1, c])
 
     def cot_begin(c):
         own_cot(c).start()
         cot_start(c)
 
     cot_begin(0)
-    cot_begin(1)
 
     vectors[...] = jnp.zeros((16, WIDTH), F32)
     low_half = lax.broadcasted_iota(jnp.int32, (CHUNKS, BLOCK, 128), 2) < 64
@@ -595,11 +595,7 @@
 
         @pl.when(c == 1)
         def _():
-            cot_begin(2)
-
-        @pl.when(c == 3)
-        def _():
-            cot_begin(3)
+            cot_begin(1)
 
     def reduction(number, part, one, two, three, done, cut):
         def remote(source, target, index, where):
@@ -760,6 +756,14 @@
 
     @pl.loop(0, CHUNKS)
     def _(c):
+        @pl.when(c == 0)
+        def _():
+            cot_begin(2)
+
+        @pl.when(c == 1)
+        def _():
+            cot_begin(3)
+
         first_wait_recv(c)
 
         @pl.when(c == 3)
@@ -1151,8 +1155,8 @@
             buffer(3, SHARE, WIDTH),
             sem((CHUNKS + 10,)),
         ]
-        + [sem((CHUNKS, SWAP))] * 8
-        + [sem((CHUNKS,))]
+        + [sem((CHUNKS,))] * 8
+        + [sem((2, CHUNKS)), sem((CHUNKS,))]
         + [sem((5, 12))] * 2
         + [sem((7,))] * 2,
         compiler_params=pltpu.CompilerParams(

time: 141 us -> 138 us (0.979)
  Pallas kernels: 139 us -> 136 us
    pallas_call x1, Pallas kernels: 135 us -> 132 us  [fused_local(): pl.pallas_call(fused_kernel, name='layer', out_shape=(result(cells, BF),...]
where the time goes in v4:
time: 138 us
  Pallas kernels  136 us (99%)
  between operations  2.13 us (2%)
    pallas_call x1, Pallas kernels, fused_local(): pl.pallas_call(fused_kernel, name='layer', out_shape=(result(cells, BF),...  132 us
    pallas_call x1, Pallas kernels, fused_local(): pl.pallas_call(finish_kernel, name='results', out_shape=shapes, in_specs=...  3.79 us

profile of v4, /device:TPU:0, one launch (start us, length us, event | category | flops | bytes accessed | tf_op | source)
XLA Modules:
  0.0 137.9 jit_solution(3175297686629026869)
XLA Ops:
  1.9 132.0 %layer.1 = (bf16[8,4,32,512]{3,2,1,0:T(8,128)(2,1)}, bf16[8,4,32,512]{3,2,1,0:T(8,128)(2,1)}, bf16[4,4,64,512]{3,2,1,0:T(8,128)(2,1)}, f32[8,256]{1,0:T(8,128)}) custom-call(bf16[8,4,32,512]{3,2,1,0:T(8,128)(2,1)} %bitcast.10, bf16[8,4,32,512]{3,2,1,0:T(8,128)(2,1)} %bitcast.11, s32[1]{0:T(128)S(6)} %copy.22.sample_counts, s32[1]{0:T(128)S(6)} %copy.23.feature_counts, ...), custom_call_target="tpu_custom_call" | custom-call | tf_op jit(solution)/shard_map/layer/pallas_call | solution.py:1100
  133.9 3.8 %results.1 = (bf16[8,4,32,512]{3,2,1,0:T(8,128)(2,1)}, bf16[8,4,32,512]{3,2,1,0:T(8,128)(2,1)}, f32[2,64,1536]{2,1,0:T(8,128)}, f32[2,64,512]{2,1,0:T(8,128)}, f...) custom-call(bf16[8,4,32,512]{3,2,1,0:T(8,128)(2,1)} %get-tuple-eleme, ...), custom_call_target="tpu_custom_call" | custom-call | tf_op jit(solution)/shard_map/results/pallas_call | solution.py:1191

commit v5 on v4

--- a/solution.py
+++ b/solution.py
@@ -1032,7 +1032,11 @@
 
 
 def finish_kernel(mixed, tokens_grad, sums_hbm, small_hbm, *refs):
-    outs, (sums, small, held, sem) = refs[:10], refs[10:]
+    results, (sums, small, held, in_two, out_two, in_mlp, out_mlp, sem) = refs[:10], refs[10:]
+    outs = [*results[:2], in_two, out_two, *results[4:6], in_mlp, results[7], out_mlp, results[9]]
+    stores = [
+        pltpu.make_async_copy(outs[k], results[k], sem.at[SUMS + 9 + n]) for n, k in enumerate((8, 6, 2, 3))
+    ]
     loads = [pltpu.make_async_copy(sums_hbm.at[k], sums.at[k], sem.at[k]) for k in range(SUMS)]
     loads.append(pltpu.make_async_copy(small_hbm, small, sem.at[SUMS]))
     cells_in, cells_out = [], []
@@ -1050,22 +1054,29 @@
     for copy in loads:
         copy.wait()
     for grp in range(GRP):
+        outs[8][SHARE * grp : SHARE * grp + SHARE] = sums[1, grp].astype(F32)
+    stores[0].start()
+    for grp in range(GRP):
         rows = slice(16 * grp, 16 * grp + 16)
         for part in range(4):
             cut = slice(WIDTH * part, WIDTH * part + WIDTH)
-            piece = slice(16 * part, 16 * part + 16)
-            outs[6][rows, cut] = sums[0, grp, piece].astype(F32)
-            if part < 3:
-                outs[2][1, rows, cut] = sums[2, grp, piece].astype(F32)
-                outs[2][0, rows, cut] = sums[3, grp, 16 * part + 16 : 16 * part + 32].astype(F32)
-        outs[8][SHARE * grp : SHARE * grp + SHARE] = sums[1, grp].astype(F32)
+            outs[6][rows, cut] = sums[0, grp, 16 * part : 16 * part + 16].astype(F32)
+    stores[1].start()
+    for grp in range(GRP):
+        rows = slice(16 * grp, 16 * grp + 16)
+        for part in range(3):
+            cut = slice(WIDTH * part, WIDTH * part + WIDTH)
+            outs[2][1, rows, cut] = sums[2, grp, 16 * part : 16 * part + 16].astype(F32)
+            outs[2][0, rows, cut] = sums[3, grp, 16 * part + 16 : 16 * part + 32].astype(F32)
         outs[3][1, rows] = sums[2, grp, 48:64].astype(F32)
         outs[3][0, rows] = sums[3, grp, 0:16].astype(F32)
+    stores[2].start()
+    stores[3].start()
     outs[4][...] = small[0:3, 0:64]
     outs[5][...] = small[3:6, 0:64]
     outs[7][...] = small[6:7, 0:256]
     outs[9][...] = small[7:8, 0:64]
-    for copy in cells_out:
+    for copy in cells_out + stores:
         copy.wait()
 
 
@@ -1193,12 +1204,16 @@
         name="results",
         out_shape=shapes,
         in_specs=[anywhere] * 4,
-        out_specs=(anywhere, anywhere) + (vector,) * 8,
+        out_specs=(anywhere,) * 4 + (vector,) * 2 + (anywhere, vector, anywhere, vector),
         scratch_shapes=[
             buffer(SUMS, GRP, SHARE, WIDTH),
             buffer(8, 256, kind=F32),
             buffer(2, *cells),
-            sem((SUMS + 9,)),
+            buffer(2, 64, 3 * WIDTH, kind=F32),
+            buffer(2, 64, WIDTH, kind=F32),
+            buffer(64, 4 * WIDTH, kind=F32),
+            buffer(256, WIDTH, kind=F32),
+            sem((SUMS + 13,)),
         ],
         compiler_params=pltpu.CompilerParams(vmem_limit_bytes=VMEM_LIMIT),
     )(mixed, tokens_grad, sums, small)

time: 138 us -> 138 us (level)
  no operation moved by 1% of the time
where the time goes in v5:
time: 138 us
  Pallas kernels  136 us (99%)
  between operations  2.13 us (2%)
    pallas_call x1, Pallas kernels, fused_local(): pl.pallas_call(fused_kernel, name='layer', out_shape=(result(cells, BF),...  132 us
    pallas_call x1, Pallas kernels, fused_local(): pl.pallas_call(finish_kernel, name='results', out_shape=shapes, in_specs=...  3.9 us

profile of v5, /device:TPU:0, one launch (start us, length us, event | category | flops | bytes accessed | tf_op | source)
XLA Modules:
  0.0 138.0 jit_solution(3283489416551869013)
XLA Ops:
  1.9 132.0 %layer.1 = (bf16[8,4,32,512]{3,2,1,0:T(8,128)(2,1)}, bf16[8,4,32,512]{3,2,1,0:T(8,128)(2,1)}, bf16[4,4,64,512]{3,2,1,0:T(8,128)(2,1)}, f32[8,256]{1,0:T(8,128)}) custom-call(bf16[8,4,32,512]{3,2,1,0:T(8,128)(2,1)} %bitcast.10, bf16[8,4,32,512]{3,2,1,0:T(8,128)(2,1)} %bitcast.11, s32[1]{0:T(128)S(6)} %copy.22.sample_counts, s32[1]{0:T(128)S(6)} %copy.23.feature_counts, ...), custom_call_target="tpu_custom_call" | custom-call | tf_op jit(solution)/shard_map/layer/pallas_call | solution.py:1111
  133.9 3.9 %results.1 = (bf16[8,4,32,512]{3,2,1,0:T(8,128)(2,1)}, bf16[8,4,32,512]{3,2,1,0:T(8,128)(2,1)}, f32[2,64,1536]{2,1,0:T(8,128)}, f32[2,64,512]{2,1,0:T(8,128)}, f...) custom-call(bf16[8,4,32,512]{3,2,1,0:T(8,128)(2,1)} %get-tuple-eleme, ...), custom_call_target="tpu_custom_call" | custom-call | tf_op jit(solution)/shard_map/results/pallas_call | solution.py:1202
